TPU v7x, 32 devices: a whole 2x2x4 slice. The times are simulated.
32 devices in a mesh: rows: 4 (over z), feat: 2 (over x), leaf: 4 (over y, core).
Axes of the slice: x: 2, y: 2, z: 4, core: 2. Of those that a mesh axis runs over, the one named last changes fastest.
Arguments:
- features: float32 [512, 8192], P(None, ('rows', 'feat')), may hold values from -4 to 4
- labels: int32 [8192], P(('rows', 'feat')), may hold values from 0 to 63
- weights: bfloat16 [4, 8192], P('leaf', ('rows', 'feat')), may hold values from 0.0009994507 to 4
- nodes: int32 [4, 8192], P('leaf', ('rows', 'feat')), may hold values from 0 to 1
Outputs:
- split_gain: float32 [4, 2, 512], P('leaf', None, ('rows', 'feat'))
- node_best: float32 [4, 2], P('leaf')
All inputs are finite; a program needn't handle non-finite values.
Results may differ from a plain program's by a relative error of at most 0.0003.
Values may be sent and summed in bfloat16 or wider, within the bound.
No kernel may reach another device: no remote copies, remote signals or barrier semaphores. Data moves between devices by JAX's collectives and lax.ppermute only.
A program may use at most 64 MiB of HBM per device.

v0:
```python
import math

import jax
import jax.numpy as jnp
from jax import lax
from jax.sharding import PartitionSpec as P

B = 128
C = 64
NODES = 2


def edge_table(bin_count, dtype):
    positions = jnp.arange(bin_count - 1, dtype=dtype)
    return (positions + 1.0 - bin_count // 2) * (9.0 / bin_count)


def split_scores(cumulative):
    totals = cumulative[..., -1:, :, :]
    right_side = totals - cumulative

    def ratio_sum(values):
        return jnp.sum(values * values, axis=-1) / jnp.maximum(jnp.sum(values, axis=-1), 1.0)

    split_value = ratio_sum(cumulative) + ratio_sum(right_side) - ratio_sum(totals)
    return jnp.max(split_value, axis=-2)


def build_targets(row_labels, row_weights, row_nodes):
    row_total = row_labels.shape[0]
    node_hit = row_nodes.T[:, :, None] == jnp.arange(NODES, dtype=jnp.int32)
    class_hit = (row_labels[:, None] == jnp.arange(C, dtype=jnp.int32)).astype(jnp.bfloat16)
    weighted = jnp.where(node_hit, row_weights.T[:, :, None], jnp.zeros((), jnp.bfloat16))
    target = weighted[:, :, :, None] * class_hit[:, None, None, :]
    return target.reshape(row_total, -1)


def local_histograms(columns, target):
    feature_total, row_total = columns.shape
    bin_count = B
    edge_values = edge_table(bin_count, jnp.float32)
    row_limit = max(1, (1 << 21) // (bin_count * row_total))
    group_size = math.gcd(feature_total, row_limit)

    def per_group(feature_set):
        below_edges = feature_set[:, None, :] <= edge_values[None, :, None]
        all_rows = jnp.ones((group_size, 1, row_total), jnp.bool_)
        below_mask = jnp.concatenate([below_edges, all_rows], axis=1).astype(jnp.bfloat16)
        return jnp.einsum("fbr,rk->fbk", below_mask, target, preferred_element_type=jnp.float32)

    grouped = columns.reshape(feature_total // group_size, group_size, row_total)
    results = lax.map(per_group, grouped)
    return results.reshape(feature_total, bin_count, -1)


def local(features, labels, weights, nodes):
    tree_count = weights.shape[0]
    columns = lax.all_to_all(features, ("rows", "feat"), split_axis=0, concat_axis=1, tiled=True)
    row_labels, row_nodes = (
        lax.all_gather(labels, ("rows", "feat"), axis=0, tiled=True),
        lax.all_gather(nodes, ("rows", "feat"), axis=1, tiled=True),
    )
    row_weights = lax.all_gather(weights, ("rows", "feat"), axis=1, tiled=True)
    cumulative = local_histograms(columns, build_targets(row_labels, row_weights, row_nodes))
    grouped_hist = cumulative.reshape(
        cumulative.shape[0], cumulative.shape[1], tree_count * NODES, C
    )
    scores = split_scores(grouped_hist)
    split_gain = scores.T.reshape(tree_count, NODES, -1)
    node_best = lax.pmax(jnp.max(split_gain, axis=2), ("rows", "feat"))
    return (split_gain, node_best)


def solution(mesh):
    return jax.shard_map(
        local,
        mesh=mesh,
        in_specs=(
            P(None, ("rows", "feat")),
            P(("rows", "feat")),
            P("leaf", ("rows", "feat")),
            P("leaf", ("rows", "feat")),
        ),
        out_specs=(P("leaf", None, ("rows", "feat")), P("leaf", None)),
        check_vma=False,
    )
```

profile of v0, /device:TPU:0, one launch (start us, length us, event | category | flops | bytes accessed | tf_op | source)
XLA Modules:
  0.0 295.7 jit_solution(9034038083994276298)
XLA Ops:
  0.7 7.4 %all-to-all-start = ((f32[8,64,1024]{2,1,0:T(8,128)}), f32[8,64,1024]{2,1,0:T(8,128)S(1)}, u32[]{:S(2)}, u32[]{:S(2)}) async-start(f32[8,64,1024]{2,1,0:T(8,128)} %bitcast.29), calls=%async_computation | async-start | bytes 4194304 | tf_op jit(solution)/shard_map/all_to_all | solution.py:58
  8.1 68.2 %all_gather.10 = bf16[1,8192]{1,0:T(2,128)(2,1)S(1)} all-gather(bf16[1,1024]{1,0:T(2,128)(2,1)S(1)} %copy-done), channel_id=1, replica_groups=mesh['rows'=4,'feat'=2,'leaf'=4] {'rows','feat'}, dimensions={1}, use_global_device_ids=true | all-gather | bytes 18432 | tf_op jit(solution)/shard_map/all_gather | solution.py:63
  76.3 30.4 %all_gather.11 = s32[8192]{0:T(1024)S(1)} all-gather(s32[1024]{0:T(1024)S(1)} %copy-done.1), channel_id=1, replica_groups=mesh['rows'=4,'feat'=2,'leaf'=4] {'rows','feat'}, dimensions={0}, use_global_device_ids=true | all-gather | bytes 36864 | tf_op jit(solution)/shard_map/all_gather | solution.py:60
  106.7 30.4 %all_gather.9 = s32[1,8192]{1,0:T(1,128)S(1)} all-gather(s32[1,1024]{1,0:T(1,128)S(1)} %copy-done.2), channel_id=1, replica_groups=mesh['rows'=4,'feat'=2,'leaf'=4] {'rows','feat'}, dimensions={1}, use_global_device_ids=true | all-gather | bytes 36864 | tf_op jit(solution)/shard_map/all_gather | solution.py:61
  137.4 2.5 copy.25
  139.9 3.0 %reshape.104 = f32[32,2,8192]{2,1,0:T(2,128)S(1)} reshape(f32[64,8,1024]{2,1,0:T(8,128)} %copy.25) | data formatting | bytes 4194304 | tf_op jit(solution)/shard_map/reshape | solution.py:51
  143.0 118.6 %while.11 = (s32[]{:T(128)}, f32[32,2,128,128]{2,3,1,0:T(8,128)}, f32[32,2,8192]{2,1,0:T(2,128)S(1)}, bf16[8192,64]{0,1:T(8,128)(2,1)S(1)}, bf16[8192,2]{0,1:T(2,128)(2,1)S(1)}, /*index=5*/s32[]{:T(128)}) while((s32[]{:T(128)}, f32[32,2,128,128]{2,3,1,0:T(8,128)}, f32[32,2,8192]{2,1,0:T(2,128)S(1)}, ...), condition=%wide.region_1.2_spmd.clone, body=%wide.region_0.1_spmd.clone.sunk | while | flops 540000512 | bytes 9766465 | solution.py:52
  144.5 2.1 fusion.21
  146.7 1.4 broadcast_compare_fusion.2
  148.2 2.2 fusion.21
  150.4 1.4 broadcast_compare_fusion.2
  151.9 2.2 fusion.21
  154.1 1.4 broadcast_compare_fusion.2
  155.7 2.2 fusion.21
  157.8 1.4 broadcast_compare_fusion.2
  159.4 2.2 fusion.21
  161.5 1.4 broadcast_compare_fusion.2
  163.1 2.1 fusion.21
  165.2 1.4 broadcast_compare_fusion.2
  166.8 2.2 fusion.21
  168.9 1.4 broadcast_compare_fusion.2
  170.5 2.2 fusion.21
  172.7 1.4 broadcast_compare_fusion.2
  174.2 2.2 fusion.21
  176.4 1.4 broadcast_compare_fusion.2
  177.9 2.2 fusion.21
  180.1 1.4 broadcast_compare_fusion.2
  181.6 2.2 fusion.21
  183.8 1.4 broadcast_compare_fusion.2
  185.3 2.2 fusion.21
  187.5 1.4 broadcast_compare_fusion.2
  189.0 2.2 fusion.21
  191.2 1.4 broadcast_compare_fusion.2
  192.7 2.2 fusion.21
  194.9 1.4 broadcast_compare_fusion.2
  196.4 2.1 fusion.21
  198.6 1.4 broadcast_compare_fusion.2
  200.1 2.2 fusion.21
  202.3 1.4 broadcast_compare_fusion.2
  203.8 2.2 fusion.21
  206.0 1.4 broadcast_compare_fusion.2
  207.5 2.2 fusion.21
  209.7 1.4 broadcast_compare_fusion.2
  211.2 2.2 fusion.21
  214.9 2.2 fusion.21
  218.6 2.1 fusion.21
  222.3 2.2 fusion.21
  226.0 2.2 fusion.21
  228.2 1.4 broadcast_compare_fusion.2
  229.7 2.2 fusion.21
  231.9 1.4 broadcast_compare_fusion.2
  233.5 2.2 fusion.21
  237.2 2.2 fusion.21
  240.9 2.2 fusion.21
  244.6 2.2 fusion.21
  248.3 2.1 fusion.21
  252.0 2.2 fusion.21
  255.7 2.1 fusion.21
  257.8 1.4 broadcast_compare_fusion.2
  259.4 2.2 fusion.21
  261.5 5.9 %slice_reduce_fusion = (f32[64,2]{1,0:T(8,128)S(1)}, f32[64,2]{1,0:T(8,128)S(1)}, f32[64,1,2,64]{1,3,2,0:T(8,128)}) fusion(f32[64,128,2,64]{1,3,2,0:T(8,128)} %bitcast.3), kind=kLoop, calls=%fused_computation.20 | loop fusion | flops 24320 | bytes 66560 | tf_op jit(solution)/shard_map/reduce_sum | solution.py:23
  267.5 3.0 %copy.27 = f32[64,1,2,64]{3,0,2,1:T(8,128)S(1)} copy(f32[64,1,2,64]{1,3,2,0:T(8,128)} %get-tuple-element.63) | data formatting | bytes 65536 | tf_op jit(solution)/shard_map/slice | solution.py:19
  270.5 4.3 %subtract_reduce_fusion = (f32[64,128,2]{1,2,0:T(2,128)S(1)}, f32[64,128,2]{1,2,0:T(2,128)S(1)}, f32[64,128,2]{1,2,0:T(2,128)S(1)}, f32[64,128,2]{1,2,0:T(2,128)S(1)}) fusion(f32[64,128,2,64]{1,3,2,0:T(8,128)} %bitcast.3, f32[64,2,64]{2,1,0:T(2,128)S(1)} %copy.28), kind=kLoop, calls=%fused_computation.14 | loop fusion | flops 7274496 | bytes 4489216 | tf_op jit(solution)/shard_map/reduce_sum | solution.py:23
  275.7 20.0 %pmax.7 = f32[1,2]{1,0:T(1,128)} all-reduce(f32[1,2]{1,0:T(1,128)S(1)} %bitcast.34), channel_id=1, replica_groups=mesh['rows'=4,'feat'=2,'leaf'=4] {'rows','feat'}, use_global_device_ids=true, to_apply=%region_10.11 | all-reduce | flops 2 | bytes 16 | tf_op jit(solution)/shard_map/pmax | solution.py:70
  (122 shorter events, 21.7 us)
Async XLA Ops:
  0.6 7.4 %copy-start = (bf16[1,1024]{1,0:T(2,128)(2,1)S(1)}, bf16[1,1024]{1,0:T(2,128)(2,1)}, u32[]{:S(2)}) copy-start(bf16[1,1024]{1,0:T(2,128)(2,1)} %param.8) | copy-start | bytes 6148
  0.6 75.7 %copy-start.1 = (s32[1024]{0:T(1024)S(1)}, s32[1024]{0:T(1024)}, u32[]{:S(2)}) copy-start(s32[1024]{0:T(1024)} %param.7) | copy-start | bytes 12292
  0.7 106.1 %copy-start.2 = (s32[1,1024]{1,0:T(1,128)S(1)}, s32[1,1024]{1,0:T(1,128)}, u32[]{:S(2)}) copy-start(s32[1,1024]{1,0:T(1,128)} %param.9) | copy-start | bytes 12292
  0.7 136.7 %all-to-all-start = ((f32[8,64,1024]{2,1,0:T(8,128)}), f32[8,64,1024]{2,1,0:T(8,128)S(1)}, u32[]{:S(2)}, u32[]{:S(2)}) async-start(f32[8,64,1024]{2,1,0:T(8,128)} %bitcast.29), calls=%async_computation | async-start | bytes 4194304 | tf_op jit(solution)/shard_map/all_to_all | solution.py:58
where the time goes:
time: 296 us
  blocking collectives  149 us (50%)
  matrix products  69.1 us (23%)
  other arithmetic  59.5 us (20%)
  local copies, waits for them, and re-layouts  9.43 us (3%)
  starting transfers between devices  7.4 us (2%)
    dot_general x32, matrix products, per_group(): jnp.einsum('fbr,rk->fbk', below_mask, target, preferred_element_type=jnp....  69.1 us
    all_gather x1, blocking collectives, local(): row_weights = lax.all_gather(weights, ('rows', 'feat'), axis=1, tiled=True)  68.2 us
    le x32, other arithmetic, per_group(): below_edges = feature_set[:, None, :] <= edge_values[None, :, None]  43.4 us
    all_gather x1, blocking collectives, local(): lax.all_gather(labels, ('rows', 'feat'), axis=0, tiled=True)  30.4 us
    all_gather x1, blocking collectives, local(): lax.all_gather(nodes, ('rows', 'feat'), axis=1, tiled=True)  30.4 us
    pmax x1, blocking collectives, local(): node_best = lax.pmax(jnp.max(split_gain, axis=2), ('rows', 'feat'))  20 us
    reduce_sum x2, other arithmetic, ratio_sum(): jnp.sum(values, axis=-1)  10.2 us
    all_to_all x1, starting transfers between devices, local(): lax.all_to_all(features, ('rows', 'feat'), split_axis=0, concat_axis=1, t...  7.4 us
  transfers between devices with their start and end apart: 1, of which 0 were waited for; matrix products, arithmetic and copies ran while one was open for 0% of the time, Pallas kernels for 0%

commit v1 on v0

v1 whole, which is shorter than its diff:
```python
import functools

import jax
import jax.numpy as jnp
from jax import lax
from jax.experimental import pallas as pl
from jax.experimental.pallas import tpu as pltpu
from jax.sharding import PartitionSpec as P

B = 128
C = 64
NODES = 2
STEP = 9.0 / B
LANES = 128
ALL = ("rows", "feat", "leaf")
BF16 = jnp.bfloat16
F32 = jnp.float32


def bin_index(values):
    nearest = jnp.round(values * (1.0 / STEP))
    above = jnp.where(values > nearest * STEP, 1.0, 0.0)
    return jnp.clip(nearest + above + (B // 2 - 1), 0.0, B - 1.0)


def score_kernel(places, sizes, msg_ref, gain_ref, target, total):
    blocks, chunks, trees, own = sizes
    feature_at, weight_at, node_at, label_at = places
    bins = lax.broadcasted_iota(jnp.int32, (B, LANES), 0).astype(F32)
    classes = lax.broadcasted_iota(jnp.int32, (C, LANES), 0).astype(F32)
    total[...] = jnp.zeros_like(total)

    def row(block, place):
        leaf, at = place
        return msg_ref[block, leaf, at : at + 1, :].astype(F32)

    def per_block(block, carry):
        for u in range(chunks):
            hit = row(block, label_at(u)) == classes
            for t in range(trees):
                weight, node = row(block, weight_at(t, u)), row(block, node_at(t, u))
                for n in range(NODES):
                    part = jnp.where(node == n, weight, 0.0)
                    at = (t * NODES + n) * C
                    target[at : at + C, u * LANES : (u + 1) * LANES] = jnp.where(hit, part, 0.0).astype(BF16)
        for f in range(own):
            below = jnp.concatenate(
                [jnp.where(row(block, feature_at(f, u)) <= bins, 1.0, 0.0).astype(BF16) for u in range(chunks)], axis=1
            )
            total[:, f * B : (f + 1) * B] += lax.dot_general(
                target[...], below, (((1,), (1,)), ((), ())), preferred_element_type=F32
            )
        return carry

    lax.fori_loop(0, blocks, per_block, 0)

    def ratio(values):
        return jnp.sum(values * values, axis=0, keepdims=True) / jnp.maximum(
            jnp.sum(values, axis=0, keepdims=True), 1.0
        )

    for k in range(trees * NODES):
        for f in range(own):
            left = total[k * C : (k + 1) * C, f * B : (f + 1) * B]
            whole = left[:, B - 1 :]
            gain = ratio(left) + ratio(whole - left) - ratio(whole)
            gain_ref[k : k + 1, f : f + 1] = jnp.max(gain, axis=1, keepdims=True)


def local(features, labels, weights, nodes, *, blocks, trees):
    feature_total, rows = features.shape
    own = feature_total // (blocks * trees)
    devices = blocks * trees
    leaf = lax.axis_index("leaf")
    if rows % LANES:
        raise ValueError("rows a device")
    chunks = rows // LANES
    split_features = own % trees == 0 and chunks % trees == 0
    if split_features:
        piece = own // trees
        mine = lax.dynamic_index_in_dim(features.reshape(blocks, trees, own, rows), leaf, 1, keepdims=False)
        binned = bin_index(mine).astype(BF16).reshape(devices, piece * chunks, LANES)
        quarter = lax.dynamic_slice_in_dim(labels, leaf * (rows // trees), rows // trees, 0)
        common = jnp.concatenate(
            [
                weights.reshape(chunks, LANES),
                nodes.astype(BF16).reshape(chunks, LANES),
                quarter.astype(BF16).reshape(chunks // trees, LANES),
            ],
            axis=0,
        )
        message = jnp.concatenate([binned, jnp.broadcast_to(common, (devices,) + common.shape)], axis=1)
        message = lax.all_to_all(message, ALL, 0, 0, tiled=True)
        message = message.reshape((blocks, trees) + message.shape[1:])
        share = chunks // trees
        places = (
            lambda f, u: (f // piece, (f % piece) * chunks + u),
            lambda t, u: (t, piece * chunks + u),
            lambda t, u: (t, (piece + 1) * chunks + u),
            lambda u: (u // share, (piece + 2) * chunks + u % share),
        )
    else:
        share = rows // trees
        mine = lax.dynamic_slice_in_dim(features, leaf * share, share, 1)
        binned = bin_index(mine).astype(BF16).reshape(devices, own * share)
        quarter = lax.dynamic_slice_in_dim(labels, leaf * share, share, 0)
        common = jnp.concatenate([weights[0], nodes[0].astype(BF16), quarter.astype(BF16)])
        message = jnp.concatenate([binned, jnp.broadcast_to(common, (devices, common.shape[0]))], axis=1)
        message = lax.all_to_all(message, ALL, 0, 0, tiled=True).reshape(blocks, trees, -1)
        ends = (own * share, own * share + rows, own * share + 2 * rows)
        parts = [
            message[:, :, : ends[0]].reshape(blocks, trees, own, share).transpose(0, 2, 1, 3),
            message[:, :, ends[0] : ends[1]],
            message[:, :, ends[1] : ends[2]],
            message[:, :, ends[2] :],
        ]
        message = jnp.concatenate([p.reshape(blocks, -1, LANES) for p in parts], axis=1)[:, None]
        places = (
            lambda f, u: (0, f * chunks + u),
            lambda t, u: (0, (own + t) * chunks + u),
            lambda t, u: (0, (own + trees + t) * chunks + u),
            lambda u: (0, (own + 2 * trees) * chunks + u),
        )
    sizes = (blocks, chunks, trees, own)
    columns = trees * NODES * C
    gains = pl.pallas_call(
        functools.partial(score_kernel, places, sizes),
        out_shape=jax.ShapeDtypeStruct((trees * NODES, own), F32),
        in_specs=[pl.BlockSpec(memory_space=pltpu.VMEM)],
        out_specs=pl.BlockSpec(memory_space=pltpu.VMEM),
        scratch_shapes=[pltpu.VMEM((columns, rows), BF16), pltpu.VMEM((columns, own * B), F32)],
        compiler_params=pltpu.CompilerParams(vmem_limit_bytes=40 << 20),
    )(message)
    outgoing = jnp.broadcast_to(gains.reshape(1, trees, NODES * own), (blocks, trees, NODES * own))
    scores = lax.all_to_all(outgoing.reshape(devices, NODES * own), ALL, 0, 0, tiled=True)
    scores = scores.reshape(blocks, trees, NODES, own)
    here = lax.axis_index("rows") * lax.axis_size("feat") + lax.axis_index("feat")
    block = lax.dynamic_index_in_dim(scores, here, 0, keepdims=False)
    if split_features:
        split_gain = block.reshape(trees, NODES, trees, own // trees).transpose(1, 2, 0, 3)
    else:
        split_gain = block.transpose(1, 0, 2)
    return split_gain.reshape(1, NODES, trees * own), jnp.max(scores, axis=(0, 1, 3)).reshape(1, NODES)


def solution(mesh):
    shape = mesh.shape
    return jax.shard_map(
        functools.partial(local, blocks=shape["rows"] * shape["feat"], trees=shape["leaf"]),
        mesh=mesh,
        in_specs=(
            P(None, ("rows", "feat")),
            P(("rows", "feat")),
            P("leaf", ("rows", "feat")),
            P("leaf", ("rows", "feat")),
        ),
        out_specs=(P("leaf", None, ("rows", "feat")), P("leaf", None)),
        check_vma=False,
    )
```

time: 296 us -> 86.8 us (0.29)
  blocking collectives: 149 us -> 21.5 us
  matrix products: 69.1 us -> 0 us
  other arithmetic: 59.5 us -> 3.19 us
  Pallas kernels: 0 us -> 48.1 us
  waiting for transfers between devices: 0.01 us -> 7.14 us
  local copies, waits for them, and re-layouts: 9.43 us -> 3.03 us
  starting transfers between devices: 7.4 us -> 2.86 us
    all_gather x3 -> x0, blocking collectives: 129 us -> none  [the longest x1 68.2 us: local(): row_weights = lax.all_gather(weights, ('rows', 'feat'), axis=1, tiled=True)]
    dot_general x32 -> x0, matrix products: 69.1 us -> none  [per_group(): jnp.einsum('fbr,rk->fbk', below_mask, target, preferred_element_type=jnp....]
    pallas_call x0 -> x1, Pallas kernels: none -> 48.1 us  [local(): pl.pallas_call(functools.partial(score_kernel, places, sizes), out_shape=...]
    le x32 -> x0, other arithmetic: 43.4 us -> none  [per_group(): below_edges = feature_set[:, None, :] <= edge_values[None, :, None]]
    all_to_all x0 -> x1, blocking collectives: none -> 21.5 us  [local(): message = lax.all_to_all(message, ALL, 0, 0, tiled=True)]
    pmax x1 -> x0, blocking collectives: 20 us -> none  [local(): node_best = lax.pmax(jnp.max(split_gain, axis=2), ('rows', 'feat'))]
    reduce_sum x2 -> x0, other arithmetic: 10.2 us -> none  [ratio_sum(): jnp.sum(values, axis=-1)]
    all_to_all x1, waiting for transfers between devices: 0.01 us -> 7.14 us  [local(): lax.all_to_all(outgoing.reshape(devices, NODES * own), ALL, 0, 0, tiled=T...]
  transfers between devices with their start and end apart: 1 -> 1, of which waited for: 0 -> 1; matrix products, arithmetic and copies ran while one was open for 0% -> 0% of each run, Pallas kernels for 0% -> 0%
where the time goes in v1:
time: 86.8 us; the launch traced here: 86.5 us
  Pallas kernels  48.1 us (55%)
  blocking collectives  21.5 us (25%)
  waiting for transfers between devices  7.14 us (8%)
  other arithmetic  3.19 us (4%)
  local copies, waits for them, and re-layouts  3.03 us (3%)
  starting transfers between devices  2.86 us (3%)
    pallas_call x1, Pallas kernels, local(): pl.pallas_call(functools.partial(score_kernel, places, sizes), out_shape=...  48.1 us
    all_to_all x1, blocking collectives, local(): message = lax.all_to_all(message, ALL, 0, 0, tiled=True)  21.5 us
    all_to_all x1, waiting for transfers between devices, local(): lax.all_to_all(outgoing.reshape(devices, NODES * own), ALL, 0, 0, tiled=T...  7.14 us
    all_to_all x1, starting transfers between devices, local(): lax.all_to_all(outgoing.reshape(devices, NODES * own), ALL, 0, 0, tiled=T...  2.86 us
  transfers between devices with their start and end apart: 1, of which 1 were waited for; matrix products, arithmetic and copies ran while one was open for 0% of the time, Pallas kernels for 0%

profile of v1, /device:TPU:0, one launch (start us, length us, event | category | flops | bytes accessed | tf_op | source)
XLA Modules:
  0.0 86.5 jit_solution(3235280636322394040)
XLA Ops:
  0.6 0.0 copy-start
  0.6 0.0 copy-start.1
  0.7 0.9 convert_reduce_fusion
  1.5 0.7 copy-done
  2.3 0.1 squeeze.6
  2.4 0.2 clamp_convert_fusion
  2.5 0.8 fusion
  3.3 0.0 copy-done.1
  3.4 21.5 %all_to_all.14 = bf16[32,50,128]{2,1,0:T(8,128)(2,1)S(1)} all-to-all(bf16[32,50,128]{2,1,0:T(8,128)(2,1)S(1)} %pad_maximum_fusion), channel_id=1, replica_groups=mesh['rows'=4,'feat'=2,'leaf'=4] {'rows','feat','leaf'}, dimensions={0} | all-to-all | bytes 819200 | tf_op jit(solution)/shard_map/all_to_all | solution.py:93
  24.9 48.1 %shard_map.59 = f32[8,16]{1,0:T(8,128)S(1)} custom-call(bf16[8,4,50,128]{3,2,1,0:T(8,128)(2,1)S(1)} %bitcast.12), custom_call_target="tpu_custom_call" | custom-call | tf_op jit(solution)/shard_map/pallas_call | solution.py:126
  73.0 0.1 broadcast_in_dim.18
  73.1 0.6 broadcast_in_dim.19
  73.7 2.9 %all-to-all-start.1 = ((f32[32,1,32]{2,1,0:T(1,128)}), f32[32,1,32]{2,1,0:T(1,128)S(1)}, u32[]{:S(2)}, u32[]{:S(2)}) async-start(f32[32,1,32]{2,1,0:T(1,128)} %bitcast.3), calls=%async_computation.1 | async-start | bytes 32768 | tf_op jit(solution)/shard_map/all_to_all | solution.py:135
  76.5 7.1 %all-to-all-done.1 = f32[32,1,32]{2,1,0:T(1,128)S(1)} async-done(((f32[32,1,32]{2,1,0:T(1,128)}), f32[32,1,32]{2,1,0:T(1,128)S(1)}, u32[]{:S(2)}, u32[]{:S(2)}) %all-to-all-start.1) | async-done | bytes 4128 | tf_op jit(solution)/shard_map/all_to_all | solution.py:135
  83.7 0.5 broadcast.12
  84.2 0.7 fusion.1
  84.9 0.1 reshape.47
  85.0 0.1 reshape.48
  85.1 0.7 reshape.49
  85.8 0.1 reduce_max.14
  85.9 0.6 reduce_max.18
  (7 shorter events, 0.2 us)
Async XLA Ops:
  0.6 1.6 %copy-start = (f32[512,1024]{1,0:T(8,128)S(1)}, f32[512,1024]{1,0:T(8,128)}, u32[]{:S(2)}) copy-start(f32[512,1024]{1,0:T(8,128)} %param.4) | copy-start | bytes 6291460
  0.6 2.7 %copy-start.1 = (bf16[1,1024]{1,0:T(2,128)(2,1)S(1)}, bf16[1,1024]{1,0:T(2,128)(2,1)}, u32[]{:S(2)}) copy-start(bf16[1,1024]{1,0:T(2,128)(2,1)} %param.6) | copy-start | bytes 6148
  73.7 10.0 %all-to-all-start.1 = ((f32[32,1,32]{2,1,0:T(1,128)}), f32[32,1,32]{2,1,0:T(1,128)S(1)}, u32[]{:S(2)}, u32[]{:S(2)}) async-start(f32[32,1,32]{2,1,0:T(1,128)} %bitcast.3), calls=%async_computation.1 | async-start | bytes 32768 | tf_op jit(solution)/shard_map/all_to_all | solution.py:135

commit v2 on v1

v2 whole, which is shorter than its diff:
```python
import functools

import jax
import jax.numpy as jnp
from jax import lax
from jax.experimental import pallas as pl
from jax.experimental.pallas import tpu as pltpu
from jax.sharding import PartitionSpec as P

B = 128
C = 64
NODES = 2
STEP = 9.0 / B
LANES = 128
GROUP = 8
SPAN = 24
ALL = ("rows", "feat", "leaf")
BF16 = jnp.bfloat16
F32 = jnp.float32
VMEM = pl.BlockSpec(memory_space=pltpu.VMEM)


def bin_index(values):
    nearest = jnp.round(values * (1.0 / STEP))
    above = jnp.where(values > nearest * STEP, 1.0, 0.0)
    return jnp.clip(nearest + above + (B // 2 - 1), 0.0, B - 1.0)


def iota(shape, axis):
    return lax.broadcasted_iota(jnp.int32, shape, axis).astype(F32)


def dot_lanes(a, b):
    return lax.dot_general(a, b, (((1,), (1,)), ((), ())), preferred_element_type=F32)


def sort_kernel(sizes, leaf_ref, feature_ref, label_ref, weight_ref, node_ref, out_ref, slab, held, ordered, packed, sem):
    blocks, trees, own, rows, chunks, piece = sizes
    devices = blocks * trees
    copy = pltpu.make_async_copy(feature_ref.at[:, leaf_ref[0]], slab, sem)
    copy.start()
    label = label_ref[...].astype(F32)
    classes = iota((C, LANES), 0)
    hits, less = [], jnp.zeros((C, LANES), F32)
    for u in range(chunks):
        part = label[:, u * LANES : (u + 1) * LANES]
        hits.append(jnp.where(part == classes, 1.0, 0.0))
        less = less + jnp.where(part < classes, 1.0, 0.0)
    lower = jnp.where(iota((LANES, LANES), 0) < iota((LANES, LANES), 1), 1.0, 0.0)
    counter = jnp.concatenate([lower, jnp.ones((LANES, LANES), F32)], axis=1).astype(BF16)
    counts = jnp.dot(
        jnp.concatenate(hits + [less], axis=0).astype(BF16), counter, preferred_element_type=F32
    )
    first = counts[chunks * C :, LANES:]
    ranks = []
    for u in range(chunks):
        within = counts[u * C : (u + 1) * C]
        ranks.append(jnp.sum(hits[u] * (first + within[:, :LANES]), axis=0, keepdims=True))
        first = first + within[:, LANES:]
    spots = iota((rows, LANES), 0)
    order = jnp.concatenate([jnp.where(rank == spots, 1.0, 0.0).astype(BF16) for rank in ranks], axis=1)
    held[devices * piece :, :] = jnp.concatenate(
        [weight_ref[...].astype(F32), node_ref[...].astype(F32), label, jnp.zeros((13, rows), F32)], axis=0
    ).astype(BF16)
    copy.wait()
    held[: devices * piece, :] = bin_index(slab[...].reshape(devices * piece, rows)).astype(BF16)
    sorted_rows = dot_lanes(held[...], order)
    for u in range(chunks):
        ordered[u] = sorted_rows[:, u * LANES : (u + 1) * LANES]
    deep = (piece + 3) * chunks
    for u in range(chunks):
        for k in range(piece):
            packed[pl.ds(k * chunks + u, devices, stride=deep), :] = ordered[u, pl.ds(k, devices, stride=piece), :]
    for k in range(3):
        tile = jnp.concatenate([ordered[u, devices * piece + k : devices * piece + k + 1, :] for u in range(chunks)], axis=0)
        for d in range(devices):
            at = d * deep + (piece + k) * chunks
            packed[at : at + chunks, :] = tile
    for d in range(devices):
        out_ref[d] = packed[d * deep : (d + 1) * deep, :].astype(BF16)


def score_kernel(places, sizes, msg_ref, gain_ref, message, target, total, whole, low, high):
    blocks, chunks, trees, own = sizes
    feature_at, weight_at, node_at, label_at = places
    wide = 2
    windows, groups = chunks // wide, blocks // GROUP
    depth = trees * NODES
    together = 2 if own % 2 == 0 else 1
    message[...] = msg_ref[...].astype(F32)
    total[...] = jnp.zeros_like(total)

    def row(block, place):
        return message[block, place[0], pl.ds(place[1], 1), :]

    def span(step, carry):
        group, w = step // windows, step % windows
        found = [row(group * GROUP + g, label_at(w * wide + u)) for g in range(GROUP) for u in range(wide)]
        found = jnp.concatenate(found, axis=0).astype(jnp.int32)
        low[step] = jnp.min(found)
        high[step] = jnp.max(found)
        return carry

    lax.fori_loop(0, groups * windows, span, 0)
    bins = iota((B, LANES), 0).astype(BF16)
    one, zero = jnp.ones((), BF16), jnp.zeros((), BF16)

    def window(step, carry):
        group, w = step // windows, step % windows
        places_in = [(group * GROUP + g, w * wide + u) for g in range(GROUP) for u in range(wide)]

        def one_pass(p, inner):
            base = low[step] + p * SPAN
            for at, (block, u) in enumerate(places_in):
                label = row(block, label_at(u)) - base.astype(F32)
                pairs = []
                for t in range(trees):
                    weight, node = row(block, weight_at(t, u)), row(block, node_at(t, u))
                    pairs += [jnp.where(node == n, weight, 0.0) for n in range(NODES)]
                pairs = jnp.concatenate(pairs, axis=0)
                for c in range(0, SPAN, 2):
                    two = [jnp.where(label == c + more, pairs, 0.0) for more in range(2)]
                    target[c * depth : (c + 2) * depth, at * LANES : (at + 1) * LANES] = jnp.concatenate(
                        two, axis=0
                    ).astype(BF16)
            start = pl.multiple_of(base * depth, 8)
            for f in range(0, own, together):
                below = jnp.concatenate(
                    [
                        jnp.concatenate(
                            [
                                jnp.where(row(block, feature_at(f + more, u)).astype(BF16) <= bins, one, zero)
                                for block, u in places_in
                            ],
                            axis=1,
                        )
                        for more in range(together)
                    ],
                    axis=0,
                )
                total[pl.ds(start, SPAN * depth), f * B : (f + together) * B] += dot_lanes(target[...], below)
            return inner

        passes = (high[step] - low[step]) // SPAN + 1
        return lax.fori_loop(0, passes, one_pass, carry)

    lax.fori_loop(0, groups * windows, window, 0)

    def ratio(squares, sums):
        return squares / jnp.maximum(sums, 1.0)

    whole_sum, whole_square = jnp.zeros((depth, B), F32), jnp.zeros((depth, B), F32)
    for c in range(C):
        part = jnp.broadcast_to(total[c * depth : (c + 1) * depth, B - 1 : B], (depth, B))
        whole[c * depth : (c + 1) * depth, :] = part
        whole_sum, whole_square = whole_sum + part, whole_square + part * part
    whole_ratio = ratio(whole_square, whole_sum)
    for f in range(own):
        left_sum, right_sum = jnp.zeros((depth, B), F32), jnp.zeros((depth, B), F32)
        left_square, right_square = jnp.zeros((depth, B), F32), jnp.zeros((depth, B), F32)
        for c in range(C):
            left = total[c * depth : (c + 1) * depth, f * B : (f + 1) * B]
            right = whole[c * depth : (c + 1) * depth, :] - left
            left_sum, left_square = left_sum + left, left_square + left * left
            right_sum, right_square = right_sum + right, right_square + right * right
        gain = ratio(left_square, left_sum) + ratio(right_square, right_sum) - whole_ratio
        gain_ref[:, f : f + 1] = jnp.max(gain, axis=1, keepdims=True)


def local(features, labels, weights, nodes, *, blocks, trees):
    feature_total, rows = features.shape
    own = feature_total // (blocks * trees)
    devices = blocks * trees
    leaf = lax.axis_index("leaf")
    chunks = rows // LANES
    split_features = own % trees == 0
    if split_features:
        piece = own // trees
        deep = (piece + 3) * chunks
        held = devices * piece
        message = pl.pallas_call(
            functools.partial(sort_kernel, (blocks, trees, own, rows, chunks, piece)),
            out_shape=jax.ShapeDtypeStruct((devices, deep, LANES), BF16),
            in_specs=[
                pl.BlockSpec(memory_space=pltpu.SMEM),
                pl.BlockSpec(memory_space=pl.ANY),
                VMEM,
                VMEM,
                VMEM,
            ],
            out_specs=VMEM,
            scratch_shapes=[
                pltpu.VMEM((blocks, own, rows), F32),
                pltpu.VMEM((held + 16, rows), BF16),
                pltpu.VMEM((chunks, held + 16, LANES), F32),
                pltpu.VMEM((devices * deep, LANES), F32),
                pltpu.SemaphoreType.DMA,
            ],
            compiler_params=pltpu.CompilerParams(vmem_limit_bytes=40 << 20),
        )(leaf.reshape(1), features.reshape(blocks, trees, own, rows), labels.reshape(1, rows), weights, nodes)
        message = lax.all_to_all(message, ALL, 0, 0, tiled=True)
        message = message.reshape(blocks, trees, deep, LANES)
        places = (
            lambda f, u: (f // piece, (f % piece) * chunks + u),
            lambda t, u: (t, piece * chunks + u),
            lambda t, u: (t, (piece + 1) * chunks + u),
            lambda u: (0, (piece + 2) * chunks + u),
        )
    else:
        share = rows // trees
        mine = lax.dynamic_slice_in_dim(features, leaf * share, share, 1)
        binned = bin_index(mine).astype(BF16).reshape(devices, own * share)
        quarter = lax.dynamic_slice_in_dim(labels, leaf * share, share, 0)
        common = jnp.concatenate([weights[0], nodes[0].astype(BF16), quarter.astype(BF16)])
        message = jnp.concatenate([binned, jnp.broadcast_to(common, (devices, common.shape[0]))], axis=1)
        message = lax.all_to_all(message, ALL, 0, 0, tiled=True).reshape(blocks, trees, -1)
        ends = (own * share, own * share + rows, own * share + 2 * rows)
        parts = [
            message[:, :, : ends[0]].reshape(blocks, trees, own, share).transpose(0, 2, 1, 3),
            message[:, :, ends[0] : ends[1]],
            message[:, :, ends[1] : ends[2]],
            message[:, :, ends[2] :],
        ]
        message = jnp.concatenate([p.reshape(blocks, -1, LANES) for p in parts], axis=1)[:, None]
        places = (
            lambda f, u: (0, f * chunks + u),
            lambda t, u: (0, (own + t) * chunks + u),
            lambda t, u: (0, (own + trees + t) * chunks + u),
            lambda u: (0, (own + 2 * trees) * chunks + u),
        )
    sizes = (blocks, chunks, trees, own)
    depth = trees * NODES
    steps = blocks * chunks // (2 * GROUP)
    gains = pl.pallas_call(
        functools.partial(score_kernel, places, sizes),
        out_shape=jax.ShapeDtypeStruct((depth, own), F32),
        in_specs=[VMEM],
        out_specs=VMEM,
        scratch_shapes=[
            pltpu.VMEM(message.shape, F32),
            pltpu.VMEM((SPAN * depth, 2 * GROUP * LANES), BF16),
            pltpu.VMEM(((C + SPAN) * depth, own * B), F32),
            pltpu.VMEM((C * depth, B), F32),
            pltpu.SMEM((steps,), jnp.int32),
            pltpu.SMEM((steps,), jnp.int32),
        ],
        compiler_params=pltpu.CompilerParams(vmem_limit_bytes=40 << 20),
    )(message)
    outgoing = jnp.broadcast_to(gains.reshape(1, trees, NODES * own), (blocks, trees, NODES * own))
    scores = lax.all_to_all(outgoing.reshape(devices, NODES * own), ALL, 0, 0, tiled=True)
    scores = scores.reshape(blocks, trees, NODES, own)
    here = lax.axis_index("rows") * lax.axis_size("feat") + lax.axis_index("feat")
    block = lax.dynamic_index_in_dim(scores, here, 0, keepdims=False)
    if split_features:
        split_gain = block.reshape(trees, NODES, trees, own // trees).transpose(1, 2, 0, 3)
    else:
        split_gain = block.transpose(1, 0, 2)
    return split_gain.reshape(1, NODES, trees * own), jnp.max(scores, axis=(0, 1, 3)).reshape(1, NODES)


def solution(mesh):
    shape = mesh.shape
    return jax.shard_map(
        functools.partial(local, blocks=shape["rows"] * shape["feat"], trees=shape["leaf"]),
        mesh=mesh,
        in_specs=(
            P(None, ("rows", "feat")),
            P(("rows", "feat")),
            P("leaf", ("rows", "feat")),
            P("leaf", ("rows", "feat")),
        ),
        out_specs=(P("leaf", None, ("rows", "feat")), P("leaf", None)),
        check_vma=False,
    )
```

time: 86.8 us -> 55 us (0.63)
  Pallas kernels: 48.1 us -> 15.5 us
  local copies, waits for them, and re-layouts: 3.03 us -> 5.77 us
  other arithmetic: 3.19 us -> 1.33 us
    pallas_call x1, Pallas kernels: 48.1 us -> 14.2 us  [local(): pl.pallas_call(functools.partial(score_kernel, places, sizes), out_shape=...]
    unnamed x4 -> x8, local copies, waits for them, and re-layouts: 0.74 us -> 3.64 us
    pallas_call x0 -> x1, Pallas kernels: none -> 1.3 us  [local(): pl.pallas_call(functools.partial(sort_kernel, (blocks, trees, own, rows,...]
    convert_element_type x2 -> x0, other arithmetic: 1.01 us -> none  [the longest x1 0.85 us: local(): nodes.astype(BF16).reshape(chunks, LANES)]
where the time goes in v2:
time: 55 us; the launch traced here: 54.7 us
  blocking collectives  21.5 us (39%)
  Pallas kernels  15.5 us (28%)
  waiting for transfers between devices  7.14 us (13%)
  local copies, waits for them, and re-layouts  5.77 us (10%)
  starting transfers between devices  2.86 us (5%)
  other arithmetic  1.33 us (2%)
  between operations  0.69 us (1%)
    all_to_all x1, blocking collectives, local(): message = lax.all_to_all(message, ALL, 0, 0, tiled=True)  21.5 us
    pallas_call x1, Pallas kernels, local(): pl.pallas_call(functools.partial(score_kernel, places, sizes), out_shape=...  14.2 us
    all_to_all x1, waiting for transfers between devices, local(): lax.all_to_all(outgoing.reshape(devices, NODES * own), ALL, 0, 0, tiled=T...  7.14 us
    unnamed x8, local copies, waits for them, and re-layouts  3.64 us
    all_to_all x1, starting transfers between devices, local(): lax.all_to_all(outgoing.reshape(devices, NODES * own), ALL, 0, 0, tiled=T...  2.86 us
    reduce_max x2, other arithmetic, local(): jnp.max(scores, axis=(0, 1, 3)).reshape(1, NODES)  1.33 us
    pallas_call x1, Pallas kernels, local(): pl.pallas_call(functools.partial(sort_kernel, (blocks, trees, own, rows,...  1.3 us
  transfers between devices with their start and end apart: 1, of which 1 were waited for; matrix products, arithmetic and copies ran while one was open for 0% of the time, Pallas kernels for 0%

profile of v2, /device:TPU:0, one launch (start us, length us, event | category | flops | bytes accessed | tf_op | source)
XLA Modules:
  0.0 54.7 jit_solution(4644388538396542054)
XLA Ops:
  0.6 0.0 copy-start
  0.6 1.6 %copy-done = f32[512,1024]{1,0:T(8,128)S(1)} copy-done((f32[512,1024]{1,0:T(8,128)S(1)}, f32[512,1024]{1,0:T(8,128)}, u32[]{:S(2)}) %copy-start) | copy-done | bytes 2097176
  2.2 0.0 copy-start.1
  2.2 0.7 %copy-done.1 = s32[1024]{0:T(1024)S(1)} copy-done((s32[1024]{0:T(1024)S(1)}, s32[1024]{0:T(1024)}, u32[]{:S(2)}) %copy-start.1) | copy-done | bytes 4120
  2.9 0.0 copy-start.2
  2.9 0.7 %copy-done.2 = bf16[1,1024]{1,0:T(2,128)(2,1)S(1)} copy-done((bf16[1,1024]{1,0:T(2,128)(2,1)S(1)}, bf16[1,1024]{1,0:T(2,128)(2,1)}, u32[]{:S(2)}) %copy-start.2) | copy-done | bytes 2072
  3.6 0.0 copy-start.3
  3.6 0.7 %copy-done.3 = s32[1,1024]{1,0:T(1,128)S(1)} copy-done((s32[1,1024]{1,0:T(1,128)S(1)}, s32[1,1024]{1,0:T(1,128)}, u32[]{:S(2)}) %copy-start.3) | copy-done | bytes 4120
  4.3 1.3 %shard_map.59 = bf16[32,56,128]{2,1,0:T(8,128)(2,1)S(1)} custom-call(s32[1]{0:T(128)} %bitcast.leaf_ref, f32[8,4,16,1024]{3,2,1,0:T(8,128)S(1)} %bitcast.7, s32[1,1024]{1,0:T(1,128)S(1)} %bitcast.9, bf16[1,1024]{1,0:T(2,128)(2,1)S(1)} %copy-done.2, s32[1,1024]{1,0:T(1,128)S(1)} %copy-done.3), custom_call_target="tpu_custom_call" | custom-call | tf_op jit(solution)/shard_map/pallas_call | solution.py:181
  5.6 21.5 %all_to_all.14 = bf16[32,56,128]{2,1,0:T(8,128)(2,1)S(1)} all-to-all(bf16[32,56,128]{2,1,0:T(8,128)(2,1)S(1)} %shard_map.59), channel_id=1, replica_groups=mesh['rows'=4,'feat'=2,'leaf'=4] {'rows','feat','leaf'}, dimensions={0} | all-to-all | bytes 917504 | tf_op jit(solution)/shard_map/all_to_all | solution.py:201
  27.1 14.2 %shard_map.60 = f32[8,16]{1,0:T(8,128)S(1)} custom-call(bf16[8,4,56,128]{3,2,1,0:T(8,128)(2,1)S(1)} %bitcast.8), custom_call_target="tpu_custom_call" | custom-call | tf_op jit(solution)/shard_map/pallas_call | solution.py:234
  41.2 0.1 broadcast_in_dim.7
  41.3 0.6 %broadcast_in_dim.8 = f32[8,4,32]{2,1,0:T(4,128)} broadcast(f32[4,32]{1,0:T(4,128)S(1)} %broadcast_in_dim.7), dimensions={1,2} | broadcast | bytes 4608 | tf_op jit(solution)/shard_map/broadcast_in_dim | solution.py:249
  41.9 2.9 %all-to-all-start.1 = ((f32[32,1,32]{2,1,0:T(1,128)}), f32[32,1,32]{2,1,0:T(1,128)S(1)}, u32[]{:S(2)}, u32[]{:S(2)}) async-start(f32[32,1,32]{2,1,0:T(1,128)} %bitcast.4), calls=%async_computation.1 | async-start | bytes 32768 | tf_op jit(solution)/shard_map/all_to_all | solution.py:250
  44.8 7.1 %all-to-all-done.1 = f32[32,1,32]{2,1,0:T(1,128)S(1)} async-done(((f32[32,1,32]{2,1,0:T(1,128)}), f32[32,1,32]{2,1,0:T(1,128)S(1)}, u32[]{:S(2)}, u32[]{:S(2)}) %all-to-all-start.1) | async-done | bytes 4128 | tf_op jit(solution)/shard_map/all_to_all | solution.py:250
  51.9 0.5 broadcast.3
  52.4 0.7 %fusion = (f32[32]{0:T(128)S(1)}, f32[32,32]{1,0:T(8,128)S(1)}) fusion(f32[32,1,32]{2,1,0:T(1,128)S(1)} %all-to-all-done.1, f32[]{:T(128)} %broadcast.3), kind=kLoop, calls=%fused_computation.1 | loop fusion | flops 992 | bytes 8324 | tf_op jit(solution)/shard_map/reduce_max | solution.py:258
  53.1 0.1 reshape.41
  53.3 0.1 reshape.42
  53.4 0.7 %reshape.43 = f32[1,2,64]{2,1,0:T(2,128)} reshape(f32[2,4,4,4]{3,2,1,0:T(4,128)S(1)} %copy.7) | data formatting | bytes 1024 | tf_op jit(solution)/shard_map/reshape | solution.py:258
  54.0 0.1 reduce_max.14
  54.1 0.6 %reduce_max.18 = f32[2]{0:T(128)} reduce(f32[2,16]{1,0:T(2,128)S(1)} %reduce_max.14, f32[]{:T(128)} %constant.21.clone.1), dimensions={1}, to_apply=%region_1.2 | reduce | flops 30 | bytes 140 | tf_op jit(solution)/shard_map/reduce_max | solution.py:258
  (2 shorter events, 0.0 us)
Async XLA Ops:
  0.6 1.6 %copy-start = (f32[512,1024]{1,0:T(8,128)S(1)}, f32[512,1024]{1,0:T(8,128)}, u32[]{:S(2)}) copy-start(f32[512,1024]{1,0:T(8,128)} %param.4) | copy-start | bytes 6291460
  2.2 0.7 %copy-start.1 = (s32[1024]{0:T(1024)S(1)}, s32[1024]{0:T(1024)}, u32[]{:S(2)}) copy-start(s32[1024]{0:T(1024)} %param.5) | copy-start | bytes 12292
  2.9 0.7 %copy-start.2 = (bf16[1,1024]{1,0:T(2,128)(2,1)S(1)}, bf16[1,1024]{1,0:T(2,128)(2,1)}, u32[]{:S(2)}) copy-start(bf16[1,1024]{1,0:T(2,128)(2,1)} %weight_ref.1) | copy-start | bytes 6148
  3.6 0.7 %copy-start.3 = (s32[1,1024]{1,0:T(1,128)S(1)}, s32[1,1024]{1,0:T(1,128)}, u32[]{:S(2)}) copy-start(s32[1,1024]{1,0:T(1,128)} %node_ref.1) | copy-start | bytes 12292
  41.9 10.0 %all-to-all-start.1 = ((f32[32,1,32]{2,1,0:T(1,128)}), f32[32,1,32]{2,1,0:T(1,128)S(1)}, u32[]{:S(2)}, u32[]{:S(2)}) async-start(f32[32,1,32]{2,1,0:T(1,128)} %bitcast.4), calls=%async_computation.1 | async-start | bytes 32768 | tf_op jit(solution)/shard_map/all_to_all | solution.py:250

commit v3 on v2

--- a/solution.py
+++ b/solution.py
@@ -1,4 +1,5 @@
 import functools
+import math
 
 import jax
 import jax.numpy as jnp
@@ -11,9 +12,12 @@
 C = 64
 NODES = 2
 STEP = 9.0 / B
+LOWEST = math.ceil(-4 / STEP) + B // 2 - 1
+HIGHEST = math.ceil(4 / STEP) + B // 2 - 1
 LANES = 128
 GROUP = 8
-SPAN = 24
+UNROLLED = 8
+SPAN = 16
 ALL = ("rows", "feat", "leaf")
 BF16 = jnp.bfloat16
 F32 = jnp.float32
@@ -23,7 +27,7 @@
 def bin_index(values):
     nearest = jnp.round(values * (1.0 / STEP))
     above = jnp.where(values > nearest * STEP, 1.0, 0.0)
-    return jnp.clip(nearest + above + (B // 2 - 1), 0.0, B - 1.0)
+    return jnp.clip(nearest + above + (B // 2 - 1), float(LOWEST), float(HIGHEST))
 
 
 def iota(shape, axis):
@@ -80,91 +84,131 @@
         out_ref[d] = packed[d * deep : (d + 1) * deep, :].astype(BF16)
 
 
-def score_kernel(places, sizes, msg_ref, gain_ref, message, target, total, whole, low, high):
+def score_kernel(places, sizes, msg_ref, gain_ref, message, target, spread, total, whole, low, high):
     blocks, chunks, trees, own = sizes
     feature_at, weight_at, node_at, label_at = places
-    wide = 2
-    windows, groups = chunks // wide, blocks // GROUP
+    groups = blocks // GROUP
+    steps = groups * chunks
     depth = trees * NODES
-    together = 2 if own % 2 == 0 else 1
+    copies = LANES // own
+    tiles = -(-(HIGHEST + 1 - LOWEST) // copies)
+    first_bin = HIGHEST + 1 - tiles * copies
+    share = total.shape[0] // steps
     message[...] = msg_ref[...].astype(F32)
-    total[...] = jnp.zeros_like(total)
 
     def row(block, place):
         return message[block, place[0], pl.ds(place[1], 1), :]
 
-    def span(step, carry):
-        group, w = step // windows, step % windows
-        found = [row(group * GROUP + g, label_at(w * wide + u)) for g in range(GROUP) for u in range(wide)]
-        found = jnp.concatenate(found, axis=0).astype(jnp.int32)
-        low[step] = jnp.min(found)
-        high[step] = jnp.max(found)
+    def members(step):
+        return [step // chunks * GROUP + g for g in range(GROUP)], step % chunks
+
+    def set_target(step, base, to):
+        held, u = members(step)
+        for g, block in enumerate(held):
+            label = row(block, label_at(u)) - base
+            pairs = []
+            for t in range(trees):
+                weight, node = row(block, weight_at(t, u)), row(block, node_at(t, u))
+                pairs += [jnp.where(node == n, weight, 0.0) for n in range(NODES)]
+            pairs = jnp.concatenate(pairs, axis=0)
+            for c in range(0, SPAN, 2):
+                two = [jnp.where(label == c + more, pairs, 0.0) for more in range(2)]
+                to[c * depth : (c + 2) * depth, g * LANES : (g + 1) * LANES] = jnp.concatenate(two, axis=0).astype(BF16)
+
+    def prepare(step, carry):
+        held, u = members(step)
+        total[pl.ds(pl.multiple_of(step * share, 8), share), :] = jnp.zeros((share, total.shape[1]), F32)
+        labels = jnp.concatenate([row(block, label_at(u)) for block in held], axis=0)
+        least = jnp.min(labels)
+        low[step] = least.astype(jnp.int32)
+        high[step] = jnp.max(labels).astype(jnp.int32)
+        set_target(step, least, target.at[step])
+        for g, block in enumerate(held):
+            tile = jnp.concatenate([row(block, feature_at(f, u)) for f in range(own)], axis=0)
+            tile = jnp.concatenate([tile] * copies, axis=0)
+            spread[step, g * LANES : (g + 1) * LANES, :] = tile.T.astype(BF16)
         return carry
 
-    lax.fori_loop(0, groups * windows, span, 0)
-    bins = iota((B, LANES), 0).astype(BF16)
+    lax.fori_loop(0, steps, prepare, 0)
+    bins = (first_bin + jnp.floor(iota((GROUP * LANES, LANES), 1) * (1.0 / own))).astype(BF16)
     one, zero = jnp.ones((), BF16), jnp.zeros((), BF16)
 
-    def window(step, carry):
-        group, w = step // windows, step % windows
-        places_in = [(group * GROUP + g, w * wide + u) for g in range(GROUP) for u in range(wide)]
-
+    def add(step, start, held):
+        start = pl.multiple_of(start * depth, 8)
+        for first in range(0, tiles, 2):
+            last = min(first + 2, tiles)
+            below = [
+                jnp.where(spread[step] <= bins + float(tile * copies), one, zero)
+                for tile in range(first, last)
+            ]
+            lanes = slice(first * LANES, last * LANES)
+            total[pl.ds(start, SPAN * depth), lanes] += jnp.dot(
+                held[...], jnp.concatenate(below, axis=1), preferred_element_type=F32
+            )
+
+    def more(step, carry):
         def one_pass(p, inner):
             base = low[step] + p * SPAN
-            for at, (block, u) in enumerate(places_in):
-                label = row(block, label_at(u)) - base.astype(F32)
-                pairs = []
-                for t in range(trees):
-                    weight, node = row(block, weight_at(t, u)), row(block, node_at(t, u))
-                    pairs += [jnp.where(node == n, weight, 0.0) for n in range(NODES)]
-                pairs = jnp.concatenate(pairs, axis=0)
-                for c in range(0, SPAN, 2):
-                    two = [jnp.where(label == c + more, pairs, 0.0) for more in range(2)]
-                    target[c * depth : (c + 2) * depth, at * LANES : (at + 1) * LANES] = jnp.concatenate(
-                        two, axis=0
-                    ).astype(BF16)
-            start = pl.multiple_of(base * depth, 8)
-            for f in range(0, own, together):
-                below = jnp.concatenate(
-                    [
-                        jnp.concatenate(
-                            [
-                                jnp.where(row(block, feature_at(f + more, u)).astype(BF16) <= bins, one, zero)
-                                for block, u in places_in
-                            ],
-                            axis=1,
-                        )
-                        for more in range(together)
-                    ],
-                    axis=0,
-                )
-                total[pl.ds(start, SPAN * depth), f * B : (f + together) * B] += dot_lanes(target[...], below)
+            set_target(step, base.astype(F32), target.at[steps])
+            add(step, base, target.at[steps])
             return inner
 
-        passes = (high[step] - low[step]) // SPAN + 1
-        return lax.fori_loop(0, passes, one_pass, carry)
-
-    lax.fori_loop(0, groups * windows, window, 0)
+        return lax.fori_loop(1, (high[step] - low[step]) // SPAN + 1, one_pass, carry)
+
+    for step in range(steps) if steps <= UNROLLED else ():
+        add(step, low[step], target.at[step])
+    if steps > UNROLLED:
+        lax.fori_loop(0, steps, lambda step, carry: add(step, low[step], target.at[step]) or carry, 0)
+    lax.fori_loop(0, steps, more, 0)
 
     def ratio(squares, sums):
         return squares / jnp.maximum(sums, 1.0)
 
-    whole_sum, whole_square = jnp.zeros((depth, B), F32), jnp.zeros((depth, B), F32)
+    zeros = jnp.zeros((depth, LANES), F32)
+    whole_sum, whole_square = zeros, zeros
     for c in range(C):
-        part = jnp.broadcast_to(total[c * depth : (c + 1) * depth, B - 1 : B], (depth, B))
+        part = jnp.broadcast_to(total[c * depth : (c + 1) * depth, tiles * LANES - 1 :], (depth, LANES))
         whole[c * depth : (c + 1) * depth, :] = part
         whole_sum, whole_square = whole_sum + part, whole_square + part * part
     whole_ratio = ratio(whole_square, whole_sum)
-    for f in range(own):
-        left_sum, right_sum = jnp.zeros((depth, B), F32), jnp.zeros((depth, B), F32)
-        left_square, right_square = jnp.zeros((depth, B), F32), jnp.zeros((depth, B), F32)
+    best = jnp.full((depth, LANES), -jnp.inf, F32)
+    for tile in range(tiles):
+        left_sum, right_sum, left_square, right_square = zeros, zeros, zeros, zeros
         for c in range(C):
-            left = total[c * depth : (c + 1) * depth, f * B : (f + 1) * B]
+            left = total[c * depth : (c + 1) * depth, tile * LANES : (tile + 1) * LANES]
             right = whole[c * depth : (c + 1) * depth, :] - left
             left_sum, left_square = left_sum + left, left_square + left * left
             right_sum, right_square = right_sum + right, right_square + right * right
         gain = ratio(left_square, left_sum) + ratio(right_square, right_sum) - whole_ratio
-        gain_ref[:, f : f + 1] = jnp.max(gain, axis=1, keepdims=True)
+        best = jnp.maximum(best, gain)
+    shift = own
+    while shift < LANES:
+        best = jnp.maximum(best, pltpu.roll(best, shift, 1))
+        shift *= 2
+    gain_ref[...] = best[:, :own]
+
+
+def score(message, places, sizes):
+    blocks, chunks, trees, own = sizes
+    depth = trees * NODES
+    steps = blocks * chunks // GROUP
+    columns = -(-(HIGHEST + 1 - LOWEST) * own // LANES) * LANES
+    return pl.pallas_call(
+        functools.partial(score_kernel, places, sizes),
+        out_shape=jax.ShapeDtypeStruct((depth, own), F32),
+        in_specs=[VMEM],
+        out_specs=VMEM,
+        scratch_shapes=[
+            pltpu.VMEM(message.shape, F32),
+            pltpu.VMEM((steps + 1, SPAN * depth, GROUP * LANES), BF16),
+            pltpu.VMEM((steps, GROUP * LANES, LANES), BF16),
+            pltpu.VMEM((-(-(C + SPAN) // steps) * steps * depth, columns), F32),
+            pltpu.VMEM((C * depth, LANES), F32),
+            pltpu.SMEM((steps,), jnp.int32),
+            pltpu.SMEM((steps,), jnp.int32),
+        ],
+        compiler_params=pltpu.CompilerParams(vmem_limit_bytes=40 << 20),
+    )(message)
 
 
 def local(features, labels, weights, nodes, *, blocks, trees):
@@ -229,23 +273,7 @@
             lambda u: (0, (own + 2 * trees) * chunks + u),
         )
     sizes = (blocks, chunks, trees, own)
-    depth = trees * NODES
-    steps = blocks * chunks // (2 * GROUP)
-    gains = pl.pallas_call(
-        functools.partial(score_kernel, places, sizes),
-        out_shape=jax.ShapeDtypeStruct((depth, own), F32),
-        in_specs=[VMEM],
-        out_specs=VMEM,
-        scratch_shapes=[
-            pltpu.VMEM(message.shape, F32),
-            pltpu.VMEM((SPAN * depth, 2 * GROUP * LANES), BF16),
-            pltpu.VMEM(((C + SPAN) * depth, own * B), F32),
-            pltpu.VMEM((C * depth, B), F32),
-            pltpu.SMEM((steps,), jnp.int32),
-            pltpu.SMEM((steps,), jnp.int32),
-        ],
-        compiler_params=pltpu.CompilerParams(vmem_limit_bytes=40 << 20),
-    )(message)
+    gains = score(message, places, sizes)
     outgoing = jnp.broadcast_to(gains.reshape(1, trees, NODES * own), (blocks, trees, NODES * own))
     scores = lax.all_to_all(outgoing.reshape(devices, NODES * own), ALL, 0, 0, tiled=True)
     scores = scores.reshape(blocks, trees, NODES, own)

time: 55 us -> 50.8 us (0.924)
  Pallas kernels: 15.5 us -> 11.3 us
    pallas_call x1, Pallas kernels: 14.2 us -> 9.97 us  [score(): pl.pallas_call(functools.partial(score_kernel, places, sizes), out_shape=...]
where the time goes in v3:
time: 50.8 us; the launch traced here: 50.5 us
  blocking collectives  21.5 us (42%)
  Pallas kernels  11.3 us (22%)
  waiting for transfers between devices  7.14 us (14%)
  local copies, waits for them, and re-layouts  5.77 us (11%)
  starting transfers between devices  2.86 us (6%)
  other arithmetic  1.33 us (3%)
  between operations  0.69 us (1%)
    all_to_all x1, blocking collectives, local(): message = lax.all_to_all(message, ALL, 0, 0, tiled=True)  21.5 us
    pallas_call x1, Pallas kernels, score(): pl.pallas_call(functools.partial(score_kernel, places, sizes), out_shape=...  9.97 us
    all_to_all x1, waiting for transfers between devices, local(): lax.all_to_all(outgoing.reshape(devices, NODES * own), ALL, 0, 0, tiled=T...  7.14 us
    unnamed x8, local copies, waits for them, and re-layouts  3.64 us
    all_to_all x1, starting transfers between devices, local(): lax.all_to_all(outgoing.reshape(devices, NODES * own), ALL, 0, 0, tiled=T...  2.86 us
    reduce_max x2, other arithmetic, local(): jnp.max(scores, axis=(0, 1, 3)).reshape(1, NODES)  1.33 us
    pallas_call x1, Pallas kernels, local(): pl.pallas_call(functools.partial(sort_kernel, (blocks, trees, own, rows,...  1.29 us
  transfers between devices with their start and end apart: 1, of which 1 were waited for; matrix products, arithmetic and copies ran while one was open for 0% of the time, Pallas kernels for 0%

profile of v3, /device:TPU:0, one launch (start us, length us, event | category | flops | bytes accessed | tf_op | source)
XLA Modules:
  0.0 50.5 jit_solution(11901663016537011053)
XLA Ops:
  0.6 0.0 copy-start
  0.6 1.6 %copy-done = f32[512,1024]{1,0:T(8,128)S(1)} copy-done((f32[512,1024]{1,0:T(8,128)S(1)}, f32[512,1024]{1,0:T(8,128)}, u32[]{:S(2)}) %copy-start) | copy-done | bytes 2097176
  2.2 0.0 copy-start.1
  2.2 0.7 %copy-done.1 = s32[1024]{0:T(1024)S(1)} copy-done((s32[1024]{0:T(1024)S(1)}, s32[1024]{0:T(1024)}, u32[]{:S(2)}) %copy-start.1) | copy-done | bytes 4120
  2.9 0.0 copy-start.2
  2.9 0.7 %copy-done.2 = bf16[1,1024]{1,0:T(2,128)(2,1)S(1)} copy-done((bf16[1,1024]{1,0:T(2,128)(2,1)S(1)}, bf16[1,1024]{1,0:T(2,128)(2,1)}, u32[]{:S(2)}) %copy-start.2) | copy-done | bytes 2072
  3.6 0.0 copy-start.3
  3.6 0.7 %copy-done.3 = s32[1,1024]{1,0:T(1,128)S(1)} copy-done((s32[1,1024]{1,0:T(1,128)S(1)}, s32[1,1024]{1,0:T(1,128)}, u32[]{:S(2)}) %copy-start.3) | copy-done | bytes 4120
  4.3 1.3 %shard_map.59 = bf16[32,56,128]{2,1,0:T(8,128)(2,1)S(1)} custom-call(s32[1]{0:T(128)} %bitcast.leaf_ref, f32[8,4,16,1024]{3,2,1,0:T(8,128)S(1)} %bitcast.7, s32[1,1024]{1,0:T(1,128)S(1)} %bitcast.9, bf16[1,1024]{1,0:T(2,128)(2,1)S(1)} %copy-done.2, s32[1,1024]{1,0:T(1,128)S(1)} %copy-done.3), custom_call_target="tpu_custom_call" | custom-call | tf_op jit(solution)/shard_map/pallas_call | solution.py:225
  5.6 21.5 %all_to_all.14 = bf16[32,56,128]{2,1,0:T(8,128)(2,1)S(1)} all-to-all(bf16[32,56,128]{2,1,0:T(8,128)(2,1)S(1)} %shard_map.59), channel_id=1, replica_groups=mesh['rows'=4,'feat'=2,'leaf'=4] {'rows','feat','leaf'}, dimensions={0} | all-to-all | bytes 917504 | tf_op jit(solution)/shard_map/all_to_all | solution.py:245
  27.1 10.0 %shard_map.60 = f32[8,16]{1,0:T(8,128)S(1)} custom-call(bf16[8,4,56,128]{3,2,1,0:T(8,128)(2,1)S(1)} %bitcast.8), custom_call_target="tpu_custom_call" | custom-call | tf_op jit(solution)/shard_map/pallas_call | solution.py:196
  37.0 0.1 broadcast_in_dim.7
  37.1 0.6 %broadcast_in_dim.8 = f32[8,4,32]{2,1,0:T(4,128)} broadcast(f32[4,32]{1,0:T(4,128)S(1)} %broadcast_in_dim.7), dimensions={1,2} | broadcast | bytes 4608 | tf_op jit(solution)/shard_map/broadcast_in_dim | solution.py:277
  37.7 2.9 %all-to-all-start.1 = ((f32[32,1,32]{2,1,0:T(1,128)}), f32[32,1,32]{2,1,0:T(1,128)S(1)}, u32[]{:S(2)}, u32[]{:S(2)}) async-start(f32[32,1,32]{2,1,0:T(1,128)} %bitcast.4), calls=%async_computation.1 | async-start | bytes 32768 | tf_op jit(solution)/shard_map/all_to_all | solution.py:278
  40.6 7.1 %all-to-all-done.1 = f32[32,1,32]{2,1,0:T(1,128)S(1)} async-done(((f32[32,1,32]{2,1,0:T(1,128)}), f32[32,1,32]{2,1,0:T(1,128)S(1)}, u32[]{:S(2)}, u32[]{:S(2)}) %all-to-all-start.1) | async-done | bytes 4128 | tf_op jit(solution)/shard_map/all_to_all | solution.py:278
  47.7 0.5 %broadcast.3 = f32[]{:T(128)} broadcast(f32[]{:T(128)} %constant.27), dimensions={} | broadcast | bytes 8 | tf_op jit(solution)/shard_map/all_to_all | solution.py:278
  48.2 0.7 %fusion = (f32[32]{0:T(128)S(1)}, f32[32,32]{1,0:T(8,128)S(1)}) fusion(f32[32,1,32]{2,1,0:T(1,128)S(1)} %all-to-all-done.1, f32[]{:T(128)} %broadcast.3), kind=kLoop, calls=%fused_computation.1 | loop fusion | flops 992 | bytes 8324 | tf_op jit(solution)/shard_map/reduce_max | solution.py:286
  48.9 0.1 reshape.41
  49.1 0.1 reshape.42
  49.2 0.7 %reshape.43 = f32[1,2,64]{2,1,0:T(2,128)} reshape(f32[2,4,4,4]{3,2,1,0:T(4,128)S(1)} %copy.7) | data formatting | bytes 1024 | tf_op jit(solution)/shard_map/reshape | solution.py:286
  49.8 0.1 reduce_max.14
  49.9 0.6 %reduce_max.18 = f32[2]{0:T(128)} reduce(f32[2,16]{1,0:T(2,128)S(1)} %reduce_max.14, f32[]{:T(128)} %constant.21.clone.1), dimensions={1}, to_apply=%region_1.2 | reduce | flops 30 | bytes 140 | tf_op jit(solution)/shard_map/reduce_max | solution.py:286
  (2 shorter events, 0.0 us)
Async XLA Ops:
  0.6 1.6 %copy-start = (f32[512,1024]{1,0:T(8,128)S(1)}, f32[512,1024]{1,0:T(8,128)}, u32[]{:S(2)}) copy-start(f32[512,1024]{1,0:T(8,128)} %param.4) | copy-start | bytes 6291460
  2.2 0.7 %copy-start.1 = (s32[1024]{0:T(1024)S(1)}, s32[1024]{0:T(1024)}, u32[]{:S(2)}) copy-start(s32[1024]{0:T(1024)} %param.5) | copy-start | bytes 12292
  2.9 0.7 %copy-start.2 = (bf16[1,1024]{1,0:T(2,128)(2,1)S(1)}, bf16[1,1024]{1,0:T(2,128)(2,1)}, u32[]{:S(2)}) copy-start(bf16[1,1024]{1,0:T(2,128)(2,1)} %weight_ref.1) | copy-start | bytes 6148
  3.6 0.7 %copy-start.3 = (s32[1,1024]{1,0:T(1,128)S(1)}, s32[1,1024]{1,0:T(1,128)}, u32[]{:S(2)}) copy-start(s32[1,1024]{1,0:T(1,128)} %node_ref.1) | copy-start | bytes 12292
  37.7 10.0 %all-to-all-start.1 = ((f32[32,1,32]{2,1,0:T(1,128)}), f32[32,1,32]{2,1,0:T(1,128)S(1)}, u32[]{:S(2)}, u32[]{:S(2)}) async-start(f32[32,1,32]{2,1,0:T(1,128)} %bitcast.4), calls=%async_computation.1 | async-start | bytes 32768 | tf_op jit(solution)/shard_map/all_to_all | solution.py:278

commit v4 on v3

--- a/solution.py
+++ b/solution.py
@@ -22,6 +22,8 @@
 BF16 = jnp.bfloat16
 F32 = jnp.float32
 VMEM = pl.BlockSpec(memory_space=pltpu.VMEM)
+SMEM = pl.BlockSpec(memory_space=pltpu.SMEM)
+HBM = pl.BlockSpec(memory_space=pltpu.HBM)
 
 
 def bin_index(values):
@@ -38,12 +40,25 @@
     return lax.dot_general(a, b, (((1,), (1,)), ((), ())), preferred_element_type=F32)
 
 
-def sort_kernel(sizes, leaf_ref, feature_ref, label_ref, weight_ref, node_ref, out_ref, slab, held, ordered, packed, sem):
+def sort_kernel(sizes, leaf_ref, feature_ref, *refs):
+    label_ref, weight_ref, node_ref, out_ref, slab, labels, weights, nodes, held, ordered, packed, sems = refs
     blocks, trees, own, rows, chunks, piece = sizes
     devices = blocks * trees
-    copy = pltpu.make_async_copy(feature_ref.at[:, leaf_ref[0]], slab, sem)
-    copy.start()
-    label = label_ref[...].astype(F32)
+    copies = [
+        pltpu.make_async_copy(source, to, sems.at[k])
+        for k, (source, to) in enumerate(
+            [
+                (label_ref, labels),
+                (weight_ref, weights),
+                (node_ref, nodes),
+                (feature_ref.at[:, leaf_ref[0]], slab),
+            ]
+        )
+    ]
+    for copy in copies:
+        copy.start()
+    copies[0].wait()
+    label = labels[...].astype(F32)
     classes = iota((C, LANES), 0)
     hits, less = [], jnp.zeros((C, LANES), F32)
     for u in range(chunks):
@@ -63,10 +78,11 @@
         first = first + within[:, LANES:]
     spots = iota((rows, LANES), 0)
     order = jnp.concatenate([jnp.where(rank == spots, 1.0, 0.0).astype(BF16) for rank in ranks], axis=1)
+    for copy in copies[1:]:
+        copy.wait()
     held[devices * piece :, :] = jnp.concatenate(
-        [weight_ref[...].astype(F32), node_ref[...].astype(F32), label, jnp.zeros((13, rows), F32)], axis=0
+        [weights[...].astype(F32), nodes[...].astype(F32), label, jnp.zeros((13, rows), F32)], axis=0
     ).astype(BF16)
-    copy.wait()
     held[: devices * piece, :] = bin_index(slab[...].reshape(devices * piece, rows)).astype(BF16)
     sorted_rows = dot_lanes(held[...], order)
     for u in range(chunks):
@@ -84,7 +100,7 @@
         out_ref[d] = packed[d * deep : (d + 1) * deep, :].astype(BF16)
 
 
-def score_kernel(places, sizes, msg_ref, gain_ref, message, target, spread, total, whole, low, high):
+def score_kernel(places, sizes, direct, leaf_ref, msg_ref, gain_ref, message, target, spread, total, whole, low, high):
     blocks, chunks, trees, own = sizes
     feature_at, weight_at, node_at, label_at = places
     groups = blocks // GROUP
@@ -185,18 +201,45 @@
     while shift < LANES:
         best = jnp.maximum(best, pltpu.roll(best, shift, 1))
         shift *= 2
-    gain_ref[...] = best[:, :own]
-
-
-def score(message, places, sizes):
+    if not direct:
+        gain_ref[...] = best[:, :own]
+        return
+    piece = own // trees
+    lane = lax.broadcasted_iota(jnp.int32, (depth, LANES), 1)
+    sent = best
+    for leaf in range(trees):
+        moved = pltpu.roll(best, lax.rem((leaf_ref[0] - leaf) * piece + LANES, LANES), 1)
+        sent = jnp.where(lane // own % trees == leaf, moved, sent)
+    for t in range(trees):
+        line = jnp.where(lane[:1] < trees * own, sent[t * NODES : t * NODES + 1], sent[t * NODES + 1 : t * NODES + 2])
+        for block in range(blocks):
+            gain_ref[block * trees + t] = line
+
+
+def finish_kernel(blocks, trees, own, here_ref, msg_ref, gain_ref, best_ref):
+    piece = own // trees
+    half = trees * own
+    lane = lax.broadcasted_iota(jnp.int32, (1, LANES), 1)
+    mine = msg_ref[here_ref[0] * trees]
+    for leaf in range(1, trees):
+        mine = jnp.where(lane // piece % trees == leaf, msg_ref[here_ref[0] * trees + leaf], mine)
+    top = msg_ref[0]
+    for d in range(1, blocks * trees):
+        top = jnp.maximum(top, msg_ref[d])
+    for n in range(NODES):
+        gain_ref[0, n : n + 1, :] = mine[:, n * half : (n + 1) * half]
+        best_ref[:, n : n + 1] = jnp.max(top[:, n * half : (n + 1) * half], axis=1, keepdims=True)
+
+
+def score(message, places, sizes, direct, leaf):
     blocks, chunks, trees, own = sizes
     depth = trees * NODES
     steps = blocks * chunks // GROUP
     columns = -(-(HIGHEST + 1 - LOWEST) * own // LANES) * LANES
     return pl.pallas_call(
-        functools.partial(score_kernel, places, sizes),
-        out_shape=jax.ShapeDtypeStruct((depth, own), F32),
-        in_specs=[VMEM],
+        functools.partial(score_kernel, places, sizes, direct),
+        out_shape=jax.ShapeDtypeStruct((blocks * trees, 1, LANES) if direct else (depth, own), F32),
+        in_specs=[SMEM, VMEM],
         out_specs=VMEM,
         scratch_shapes=[
             pltpu.VMEM(message.shape, F32),
@@ -208,14 +251,14 @@
             pltpu.SMEM((steps,), jnp.int32),
         ],
         compiler_params=pltpu.CompilerParams(vmem_limit_bytes=40 << 20),
-    )(message)
+    )(leaf, message)
 
 
 def local(features, labels, weights, nodes, *, blocks, trees):
     feature_total, rows = features.shape
     own = feature_total // (blocks * trees)
     devices = blocks * trees
-    leaf = lax.axis_index("leaf")
+    leaf = lax.axis_index("leaf").reshape(1)
     chunks = rows // LANES
     split_features = own % trees == 0
     if split_features:
@@ -226,22 +269,25 @@
             functools.partial(sort_kernel, (blocks, trees, own, rows, chunks, piece)),
             out_shape=jax.ShapeDtypeStruct((devices, deep, LANES), BF16),
             in_specs=[
-                pl.BlockSpec(memory_space=pltpu.SMEM),
-                pl.BlockSpec(memory_space=pl.ANY),
-                VMEM,
-                VMEM,
-                VMEM,
+                SMEM,
+                HBM,
+                HBM,
+                HBM,
+                HBM,
             ],
             out_specs=VMEM,
             scratch_shapes=[
                 pltpu.VMEM((blocks, own, rows), F32),
+                pltpu.VMEM((1, rows), jnp.int32),
+                pltpu.VMEM((1, rows), BF16),
+                pltpu.VMEM((1, rows), jnp.int32),
                 pltpu.VMEM((held + 16, rows), BF16),
                 pltpu.VMEM((chunks, held + 16, LANES), F32),
                 pltpu.VMEM((devices * deep, LANES), F32),
-                pltpu.SemaphoreType.DMA,
+                pltpu.SemaphoreType.DMA((4,)),
             ],
-            compiler_params=pltpu.CompilerParams(vmem_limit_bytes=40 << 20),
-        )(leaf.reshape(1), features.reshape(blocks, trees, own, rows), labels.reshape(1, rows), weights, nodes)
+            compiler_params=pltpu.CompilerParams(vmem_limit_bytes=60 << 20),
+        )(leaf, features.reshape(blocks, trees, own, rows), labels.reshape(1, rows), weights, nodes)
         message = lax.all_to_all(message, ALL, 0, 0, tiled=True)
         message = message.reshape(blocks, trees, deep, LANES)
         places = (
@@ -252,9 +298,9 @@
         )
     else:
         share = rows // trees
-        mine = lax.dynamic_slice_in_dim(features, leaf * share, share, 1)
+        mine = lax.dynamic_slice_in_dim(features, leaf[0] * share, share, 1)
         binned = bin_index(mine).astype(BF16).reshape(devices, own * share)
-        quarter = lax.dynamic_slice_in_dim(labels, leaf * share, share, 0)
+        quarter = lax.dynamic_slice_in_dim(labels, leaf[0] * share, share, 0)
         common = jnp.concatenate([weights[0], nodes[0].astype(BF16), quarter.astype(BF16)])
         message = jnp.concatenate([binned, jnp.broadcast_to(common, (devices, common.shape[0]))], axis=1)
         message = lax.all_to_all(message, ALL, 0, 0, tiled=True).reshape(blocks, trees, -1)
@@ -273,11 +319,22 @@
             lambda u: (0, (own + 2 * trees) * chunks + u),
         )
     sizes = (blocks, chunks, trees, own)
-    gains = score(message, places, sizes)
+    direct = split_features and NODES * trees * own == LANES
+    here = lax.axis_index("rows") * lax.axis_size("feat") + lax.axis_index("feat")
+    gains = score(message, places, sizes, direct, leaf)
+    if direct:
+        return pl.pallas_call(
+            functools.partial(finish_kernel, blocks, trees, own),
+            out_shape=(
+                jax.ShapeDtypeStruct((1, NODES, trees * own), F32),
+                jax.ShapeDtypeStruct((1, NODES), F32),
+            ),
+            in_specs=[SMEM, VMEM],
+            out_specs=(pl.BlockSpec(), pl.BlockSpec()),
+        )(here.reshape(1), lax.all_to_all(gains, ALL, 0, 0, tiled=True))
     outgoing = jnp.broadcast_to(gains.reshape(1, trees, NODES * own), (blocks, trees, NODES * own))
     scores = lax.all_to_all(outgoing.reshape(devices, NODES * own), ALL, 0, 0, tiled=True)
     scores = scores.reshape(blocks, trees, NODES, own)
-    here = lax.axis_index("rows") * lax.axis_size("feat") + lax.axis_index("feat")
     block = lax.dynamic_index_in_dim(scores, here, 0, keepdims=False)
     if split_features:
         split_gain = block.reshape(trees, NODES, trees, own // trees).transpose(1, 2, 0, 3)

time: 50.8 us -> 48.2 us (0.949)
  local copies, waits for them, and re-layouts: 5.77 us -> 0.6 us
  Pallas kernels: 11.3 us -> 14.9 us
  other arithmetic: 1.33 us -> 0 us
    unnamed x8 -> x2, local copies, waits for them, and re-layouts: 3.64 us -> 0.6 us
    pallas_call x1 -> x2, Pallas kernels: 9.97 us -> 12 us  [the longest x1 10.7 us: score(): pl.pallas_call(functools.partial(score_kernel, places, sizes, direct), ou...]
    pallas_call x1, Pallas kernels: 1.29 us -> 2.85 us  [local(): pl.pallas_call(functools.partial(sort_kernel, (blocks, trees, own, rows,...]
    reduce_max x2 -> x0, other arithmetic: 1.33 us -> none  [local(): jnp.max(scores, axis=(0, 1, 3)).reshape(1, NODES)]
    reshape x3 -> x0, local copies, waits for them, and re-layouts: 0.83 us -> none  [the longest x1 0.66 us: local(): split_gain.reshape(1, NODES, trees * own)]
    broadcast_in_dim x2 -> x0, local copies, waits for them, and re-layouts: 0.68 us -> none  [local(): jnp.broadcast_to(gains.reshape(1, trees, NODES * own), (blocks, trees, NO...]
    all_to_all x1 -> x0, local copies, waits for them, and re-layouts: 0.51 us -> none  [local(): lax.all_to_all(outgoing.reshape(devices, NODES * own), ALL, 0, 0, tiled=T...]
where the time goes in v4:
time: 48.2 us; the launch traced here: 47.8 us
  blocking collectives  21.7 us (45%)
  Pallas kernels  14.9 us (31%)
  waiting for transfers between devices  7.14 us (15%)
  starting transfers between devices  2.85 us (6%)
  between operations  0.66 us (1%)
  local copies, waits for them, and re-layouts  0.6 us (1%)
    all_to_all x1, blocking collectives, local(): message = lax.all_to_all(message, ALL, 0, 0, tiled=True)  21.7 us
    pallas_call x1, Pallas kernels, score(): pl.pallas_call(functools.partial(score_kernel, places, sizes, direct), ou...  10.7 us
    all_to_all x1, waiting for transfers between devices, local(): lax.all_to_all(gains, ALL, 0, 0, tiled=True)  7.14 us
    all_to_all x1, starting transfers between devices, local(): lax.all_to_all(gains, ALL, 0, 0, tiled=True)  2.85 us
    pallas_call x1, Pallas kernels, local(): pl.pallas_call(functools.partial(sort_kernel, (blocks, trees, own, rows,...  2.85 us
    pallas_call x1, Pallas kernels, local(): pl.pallas_call(functools.partial(finish_kernel, blocks, trees, own), out_...  1.36 us
  transfers between devices with their start and end apart: 1, of which 1 were waited for; matrix products, arithmetic and copies ran while one was open for 0% of the time, Pallas kernels for 0%

profile of v4, /device:TPU:0, one launch (start us, length us, event | category | flops | bytes accessed | tf_op | source)
XLA Modules:
  0.0 47.8 jit_solution(5368536363427439734)
XLA Ops:
  0.6 2.9 %shard_map.59 = bf16[32,56,128]{2,1,0:T(8,128)(2,1)} custom-call(s32[1]{0:T(128)} %bitcast.1.leaf_ref, f32[8,4,16,1024]{3,2,1,0:T(8,128)} %bitcast.6, s32[1,1024]{1,0:T(1,128)} %bitcast.7, bf16[1,1024]{1,0:T(2,128)(2,1)} %refs_1_.1, s32[1,1024]{1,0:T(1,128)} %refs_2_.1), custom_call_target="tpu_custom_call" | custom-call | tf_op jit(solution)/shard_map/pallas_call | solution.py:268
  3.5 21.7 %all_to_all.10 = bf16[32,56,128]{2,1,0:T(8,128)(2,1)S(1)} all-to-all(bf16[32,56,128]{2,1,0:T(8,128)(2,1)} %shard_map.59), channel_id=1, replica_groups=mesh['rows'=4,'feat'=2,'leaf'=4] {'rows','feat','leaf'}, dimensions={0} | all-to-all | bytes 917504 | tf_op jit(solution)/shard_map/all_to_all | solution.py:291
  25.2 10.7 %shard_map.60 = f32[32,1,128]{2,1,0:T(1,128)} custom-call(s32[1]{0:T(128)} %bitcast.1.leaf_ref, bf16[8,4,56,128]{3,2,1,0:T(8,128)(2,1)S(1)} %bitcast.5), custom_call_target="tpu_custom_call" | custom-call | tf_op jit(solution)/shard_map/pallas_call | solution.py:239
  35.8 2.9 %all-to-all-start.1 = ((f32[32,1,128]{2,1,0:T(1,128)}), f32[32,1,128]{2,1,0:T(1,128)S(1)}, u32[]{:S(2)}, u32[]{:S(2)}) async-start(f32[32,1,128]{2,1,0:T(1,128)} %shard_map.60), calls=%async_computation.1 | async-start | bytes 32768 | tf_op jit(solution)/shard_map/all_to_all | solution.py:334
  38.7 7.1 %all-to-all-done.1.msg_ref = f32[32,1,128]{2,1,0:T(1,128)S(1)} async-done(((f32[32,1,128]{2,1,0:T(1,128)}), f32[32,1,128]{2,1,0:T(1,128)S(1)}, u32[]{:S(2)}, u32[]{:S(2)}) %all-to-all-start.1) | async-done | bytes 16416 | tf_op jit(solution)/shard_map/all_to_all | solution.py:334
  45.8 0.0 copy-start
  45.8 0.6 %copy-done = f32[32,1,128]{2,1,0:T(1,128)} copy-done((f32[32,1,128]{2,1,0:T(1,128)}, f32[32,1,128]{2,1,0:T(1,128)S(1)}, u32[]{:S(2)}) %copy-start) | copy-done | bytes 16408
  46.4 1.4 %shard_map.61 = (f32[1,2,64]{2,1,0:T(2,128)}, f32[1,2]{1,0:T(1,128)}) custom-call(s32[1]{0:T(128)} %bitcast.here_ref, f32[32,1,128]{2,1,0:T(1,128)} %copy-done), custom_call_target="tpu_custom_call" | custom-call | tf_op jit(solution)/shard_map/pallas_call | solution.py:326
Async XLA Ops:
  35.8 10.0 %all-to-all-start.1 = ((f32[32,1,128]{2,1,0:T(1,128)}), f32[32,1,128]{2,1,0:T(1,128)S(1)}, u32[]{:S(2)}, u32[]{:S(2)}) async-start(f32[32,1,128]{2,1,0:T(1,128)} %shard_map.60), calls=%async_computation.1 | async-start | bytes 32768 | tf_op jit(solution)/shard_map/all_to_all | solution.py:334
  45.8 0.6 %copy-start = (f32[32,1,128]{2,1,0:T(1,128)}, f32[32,1,128]{2,1,0:T(1,128)S(1)}, u32[]{:S(2)}) copy-start(f32[32,1,128]{2,1,0:T(1,128)S(1)} %all-to-all-done.1.msg_ref) | copy-start | bytes 49156

commit v5 on v4

--- a/solution.py
+++ b/solution.py
@@ -40,7 +40,7 @@
     return lax.dot_general(a, b, (((1,), (1,)), ((), ())), preferred_element_type=F32)
 
 
-def sort_kernel(sizes, leaf_ref, feature_ref, *refs):
+def sort_kernel(sizes, leaf_ref, here_ref, feature_ref, *refs):
     label_ref, weight_ref, node_ref, out_ref, slab, labels, weights, nodes, held, ordered, packed, sems = refs
     blocks, trees, own, rows, chunks, piece = sizes
     devices = blocks * trees
@@ -100,7 +100,7 @@
         out_ref[d] = packed[d * deep : (d + 1) * deep, :].astype(BF16)
 
 
-def score_kernel(places, sizes, direct, leaf_ref, msg_ref, gain_ref, message, target, spread, total, whole, low, high):
+def score_kernel(places, sizes, direct, leaf_ref, here_ref, msg_ref, gain_ref, message, target, spread, total, whole, low, high):
     blocks, chunks, trees, own = sizes
     feature_at, weight_at, node_at, label_at = places
     groups = blocks // GROUP
@@ -145,7 +145,7 @@
             spread[step, g * LANES : (g + 1) * LANES, :] = tile.T.astype(BF16)
         return carry
 
-    lax.fori_loop(0, steps, prepare, 0)
+    lax.fori_loop(0, steps, prepare, 0, unroll=4)
     bins = (first_bin + jnp.floor(iota((GROUP * LANES, LANES), 1) * (1.0 / own))).astype(BF16)
     one, zero = jnp.ones((), BF16), jnp.zeros((), BF16)
 
@@ -231,7 +231,7 @@
         best_ref[:, n : n + 1] = jnp.max(top[:, n * half : (n + 1) * half], axis=1, keepdims=True)
 
 
-def score(message, places, sizes, direct, leaf):
+def score(message, places, sizes, direct, leaf, here):
     blocks, chunks, trees, own = sizes
     depth = trees * NODES
     steps = blocks * chunks // GROUP
@@ -239,7 +239,7 @@
     return pl.pallas_call(
         functools.partial(score_kernel, places, sizes, direct),
         out_shape=jax.ShapeDtypeStruct((blocks * trees, 1, LANES) if direct else (depth, own), F32),
-        in_specs=[SMEM, VMEM],
+        in_specs=[SMEM, SMEM, VMEM],
         out_specs=VMEM,
         scratch_shapes=[
             pltpu.VMEM(message.shape, F32),
@@ -251,7 +251,7 @@
             pltpu.SMEM((steps,), jnp.int32),
         ],
         compiler_params=pltpu.CompilerParams(vmem_limit_bytes=40 << 20),
-    )(leaf, message)
+    )(leaf, here, message)
 
 
 def local(features, labels, weights, nodes, *, blocks, trees):
@@ -259,6 +259,7 @@
     own = feature_total // (blocks * trees)
     devices = blocks * trees
     leaf = lax.axis_index("leaf").reshape(1)
+    here = (lax.axis_index("rows") * lax.axis_size("feat") + lax.axis_index("feat")).reshape(1)
     chunks = rows // LANES
     split_features = own % trees == 0
     if split_features:
@@ -269,6 +270,7 @@
             functools.partial(sort_kernel, (blocks, trees, own, rows, chunks, piece)),
             out_shape=jax.ShapeDtypeStruct((devices, deep, LANES), BF16),
             in_specs=[
+                SMEM,
                 SMEM,
                 HBM,
                 HBM,
@@ -287,7 +289,7 @@
                 pltpu.SemaphoreType.DMA((4,)),
             ],
             compiler_params=pltpu.CompilerParams(vmem_limit_bytes=60 << 20),
-        )(leaf, features.reshape(blocks, trees, own, rows), labels.reshape(1, rows), weights, nodes)
+        )(leaf, here, features.reshape(blocks, trees, own, rows), labels.reshape(1, rows), weights, nodes)
         message = lax.all_to_all(message, ALL, 0, 0, tiled=True)
         message = message.reshape(blocks, trees, deep, LANES)
         places = (
@@ -320,8 +322,7 @@
         )
     sizes = (blocks, chunks, trees, own)
     direct = split_features and NODES * trees * own == LANES
-    here = lax.axis_index("rows") * lax.axis_size("feat") + lax.axis_index("feat")
-    gains = score(message, places, sizes, direct, leaf)
+    gains = score(message, places, sizes, direct, leaf, here)
     if direct:
         return pl.pallas_call(
             functools.partial(finish_kernel, blocks, trees, own),
@@ -331,11 +332,11 @@
             ),
             in_specs=[SMEM, VMEM],
             out_specs=(pl.BlockSpec(), pl.BlockSpec()),
-        )(here.reshape(1), lax.all_to_all(gains, ALL, 0, 0, tiled=True))
+        )(here, lax.all_to_all(gains, ALL, 0, 0, tiled=True))
     outgoing = jnp.broadcast_to(gains.reshape(1, trees, NODES * own), (blocks, trees, NODES * own))
     scores = lax.all_to_all(outgoing.reshape(devices, NODES * own), ALL, 0, 0, tiled=True)
     scores = scores.reshape(blocks, trees, NODES, own)
-    block = lax.dynamic_index_in_dim(scores, here, 0, keepdims=False)
+    block = lax.dynamic_index_in_dim(scores, here[0], 0, keepdims=False)
     if split_features:
         split_gain = block.reshape(trees, NODES, trees, own // trees).transpose(1, 2, 0, 3)
     else:

time: 48.2 us -> 46.6 us (0.967)
  blocking collectives: 21.7 us -> 31.5 us
  waiting for transfers between devices: 7.14 us -> 0 us
  starting transfers between devices: 2.85 us -> 0 us
  Pallas kernels: 14.9 us -> 14.1 us
  local copies, waits for them, and re-layouts: 0.6 us -> 0 us
    all_to_all x0 -> x1, blocking collectives: none -> 9.78 us  [local(): lax.all_to_all(gains, ALL, 0, 0, tiled=True)]
    all_to_all x1 -> x0, waiting for transfers between devices: 7.14 us -> none  [local(): lax.all_to_all(gains, ALL, 0, 0, tiled=True)]
    all_to_all x1 -> x0, starting transfers between devices: 2.85 us -> none  [local(): lax.all_to_all(gains, ALL, 0, 0, tiled=True)]
    pallas_call x1, Pallas kernels: 10.7 us -> 9.93 us  [score(): pl.pallas_call(functools.partial(score_kernel, places, sizes, direct), ou...]
    unnamed x2 -> x0, local copies, waits for them, and re-layouts: 0.6 us -> none
  transfers between devices with their start and end apart: 1 -> 0, of which waited for: 1 -> 0; matrix products, arithmetic and copies ran while one was open for 0% -> 0% of each run, Pallas kernels for 0% -> 0%
where the time goes in v5:
time: 46.6 us; the launch traced here: 46.2 us
  blocking collectives  31.5 us (68%)
  Pallas kernels  14.1 us (30%)
  between operations  0.65 us (1%)
    all_to_all x1, blocking collectives, local(): message = lax.all_to_all(message, ALL, 0, 0, tiled=True)  21.7 us
    pallas_call x1, Pallas kernels, score(): pl.pallas_call(functools.partial(score_kernel, places, sizes, direct), ou...  9.93 us
    all_to_all x1, blocking collectives, local(): lax.all_to_all(gains, ALL, 0, 0, tiled=True)  9.78 us
    pallas_call x1, Pallas kernels, local(): pl.pallas_call(functools.partial(sort_kernel, (blocks, trees, own, rows,...  2.84 us
    pallas_call x1, Pallas kernels, local(): pl.pallas_call(functools.partial(finish_kernel, blocks, trees, own), out_...  1.36 us

profile of v5, /device:TPU:0, one launch (start us, length us, event | category | flops | bytes accessed | tf_op | source)
XLA Modules:
  0.0 46.2 jit_solution(6701413604723158468)
XLA Ops:
  0.6 2.8 %shard_map.59 = bf16[32,56,128]{2,1,0:T(8,128)(2,1)} custom-call(s32[1]{0:T(128)} %bitcast.1.leaf_ref, s32[1]{0:T(128)} %bitcast.here_ref, f32[8,4,16,1024]{3,2,1,0:T(8,128)} %bitcast.6, s32[1,1024]{1,0:T(1,128)} %bitcast.7, bf16[1,1024]{1,0:T(2,128)(2,1)} %refs_1_.1, s32[1,1024]{1,0:T(1,128)} %refs_2_.1), custom_call_target="tpu_custom_call" | custom-call | tf_op jit(solution)/shard_map/pallas_call | solution.py:269
  3.5 21.7 %all_to_all.10 = bf16[32,56,128]{2,1,0:T(8,128)(2,1)S(1)} all-to-all(bf16[32,56,128]{2,1,0:T(8,128)(2,1)} %shard_map.59), channel_id=1, replica_groups=mesh['rows'=4,'feat'=2,'leaf'=4] {'rows','feat','leaf'}, dimensions={0} | all-to-all | bytes 917504 | tf_op jit(solution)/shard_map/all_to_all | solution.py:293
  25.2 9.9 %shard_map.60 = f32[32,1,128]{2,1,0:T(1,128)S(1)} custom-call(s32[1]{0:T(128)} %bitcast.1.leaf_ref, s32[1]{0:T(128)} %bitcast.here_ref, bf16[8,4,56,128]{3,2,1,0:T(8,128)(2,1)S(1)} %bitcast.5), custom_call_target="tpu_custom_call" | custom-call | tf_op jit(solution)/shard_map/pallas_call | solution.py:239
  35.1 9.8 %all_to_all.11.msg_ref = f32[32,1,128]{2,1,0:T(1,128)} all-to-all(f32[32,1,128]{2,1,0:T(1,128)S(1)} %shard_map.60), channel_id=1, replica_groups=mesh['rows'=4,'feat'=2,'leaf'=4] {'rows','feat','leaf'}, dimensions={0} | all-to-all | bytes 32768 | tf_op jit(solution)/shard_map/all_to_all | solution.py:335
  44.9 1.4 %shard_map.61 = (f32[1,2,64]{2,1,0:T(2,128)}, f32[1,2]{1,0:T(1,128)}) custom-call(s32[1]{0:T(128)} %bitcast.here_ref, f32[32,1,128]{2,1,0:T(1,128)} %all_to_all.11.msg_ref), custom_call_target="tpu_custom_call" | custom-call | tf_op jit(solution)/shard_map/pallas_call | solution.py:327

commit v6 on v5

--- a/solution.py
+++ b/solution.py
@@ -109,8 +109,8 @@
     copies = LANES // own
     tiles = -(-(HIGHEST + 1 - LOWEST) // copies)
     first_bin = HIGHEST + 1 - tiles * copies
-    share = total.shape[0] // steps
     message[...] = msg_ref[...].astype(F32)
+    total[: C * depth, :] = jnp.zeros((C * depth, total.shape[1]), F32)
 
     def row(block, place):
         return message[block, place[0], pl.ds(place[1], 1), :]
@@ -118,63 +118,78 @@
     def members(step):
         return [step // chunks * GROUP + g for g in range(GROUP)], step % chunks
 
-    def set_target(step, base, to):
+    def set_target(block, u, lanes, base, to):
+        label = row(block, label_at(u)) - base
+        pairs = []
+        for t in range(trees):
+            weight, node = row(block, weight_at(t, u)), row(block, node_at(t, u))
+            pairs += [jnp.where(node == n, weight, 0.0) for n in range(NODES)]
+        pairs = jnp.concatenate(pairs, axis=0)
+        for c in range(0, SPAN, 2):
+            two = [jnp.where(label == c + more, pairs, 0.0) for more in range(2)]
+            to[c * depth : (c + 2) * depth, lanes] = jnp.concatenate(two, axis=0).astype(BF16)
+
+    def set_limits(step):
         held, u = members(step)
-        for g, block in enumerate(held):
-            label = row(block, label_at(u)) - base
-            pairs = []
-            for t in range(trees):
-                weight, node = row(block, weight_at(t, u)), row(block, node_at(t, u))
-                pairs += [jnp.where(node == n, weight, 0.0) for n in range(NODES)]
-            pairs = jnp.concatenate(pairs, axis=0)
-            for c in range(0, SPAN, 2):
-                two = [jnp.where(label == c + more, pairs, 0.0) for more in range(2)]
-                to[c * depth : (c + 2) * depth, g * LANES : (g + 1) * LANES] = jnp.concatenate(two, axis=0).astype(BF16)
-
-    def prepare(step, carry):
+        labels = jnp.concatenate([row(block, label_at(u)) for block in held], axis=0)
+        low[step] = jnp.min(labels).astype(jnp.int32)
+        high[step] = jnp.max(labels).astype(jnp.int32)
+
+    def prepare(step, g):
         held, u = members(step)
-        total[pl.ds(pl.multiple_of(step * share, 8), share), :] = jnp.zeros((share, total.shape[1]), F32)
-        labels = jnp.concatenate([row(block, label_at(u)) for block in held], axis=0)
-        least = jnp.min(labels)
-        low[step] = least.astype(jnp.int32)
-        high[step] = jnp.max(labels).astype(jnp.int32)
-        set_target(step, least, target.at[step])
-        for g, block in enumerate(held):
-            tile = jnp.concatenate([row(block, feature_at(f, u)) for f in range(own)], axis=0)
-            tile = jnp.concatenate([tile] * copies, axis=0)
-            spread[step, g * LANES : (g + 1) * LANES, :] = tile.T.astype(BF16)
-        return carry
-
-    lax.fori_loop(0, steps, prepare, 0, unroll=4)
+        lanes = slice(g * LANES, (g + 1) * LANES)
+        set_target(held[g], u, lanes, low[step].astype(F32), target.at[step])
+        tile = jnp.concatenate([row(held[g], feature_at(f, u)) for f in range(own)], axis=0)
+        tile = jnp.concatenate([tile] * copies, axis=0)
+        spread[step, lanes, :] = tile.T.astype(BF16)
+
     bins = (first_bin + jnp.floor(iota((GROUP * LANES, LANES), 1) * (1.0 / own))).astype(BF16)
     one, zero = jnp.ones((), BF16), jnp.zeros((), BF16)
 
-    def add(step, start, held):
+    def add(step, start, held, beside=None):
         start = pl.multiple_of(start * depth, 8)
-        for first in range(0, tiles, 2):
+        for at, first in enumerate(range(0, tiles, 2)):
             last = min(first + 2, tiles)
             below = [
-                jnp.where(spread[step] <= bins + float(tile * copies), one, zero)
+                jnp.minimum(jnp.maximum((bins + float(tile * copies + 1)) - spread[step], zero), one)
                 for tile in range(first, last)
             ]
             lanes = slice(first * LANES, last * LANES)
             total[pl.ds(start, SPAN * depth), lanes] += jnp.dot(
                 held[...], jnp.concatenate(below, axis=1), preferred_element_type=F32
             )
+            if beside is not None:
+                for g in range(at, GROUP, -(-tiles // 2)):
+                    prepare(beside, g)
 
     def more(step, carry):
         def one_pass(p, inner):
             base = low[step] + p * SPAN
-            set_target(step, base.astype(F32), target.at[steps])
+            held, u = members(step)
+            for g in range(GROUP):
+                lanes = slice(g * LANES, (g + 1) * LANES)
+                set_target(held[g], u, lanes, base.astype(F32), target.at[steps])
             add(step, base, target.at[steps])
             return inner
 
         return lax.fori_loop(1, (high[step] - low[step]) // SPAN + 1, one_pass, carry)
 
-    for step in range(steps) if steps <= UNROLLED else ():
+    def window(step, carry):
+        set_limits(step)
+        for g in range(GROUP):
+            prepare(step, g)
         add(step, low[step], target.at[step])
-    if steps > UNROLLED:
-        lax.fori_loop(0, steps, lambda step, carry: add(step, low[step], target.at[step]) or carry, 0)
+        return carry
+
+    if steps <= UNROLLED:
+        for step in range(steps):
+            set_limits(step)
+        for g in range(GROUP):
+            prepare(0, g)
+        for step in range(steps):
+            add(step, low[step], target.at[step], step + 1 if step + 1 < steps else None)
+    else:
+        lax.fori_loop(0, steps, window, 0)
     lax.fori_loop(0, steps, more, 0)
 
     def ratio(squares, sums):
@@ -245,7 +260,7 @@
             pltpu.VMEM(message.shape, F32),
             pltpu.VMEM((steps + 1, SPAN * depth, GROUP * LANES), BF16),
             pltpu.VMEM((steps, GROUP * LANES, LANES), BF16),
-            pltpu.VMEM((-(-(C + SPAN) // steps) * steps * depth, columns), F32),
+            pltpu.VMEM(((C + SPAN) * depth, columns), F32),
             pltpu.VMEM((C * depth, LANES), F32),
             pltpu.SMEM((steps,), jnp.int32),
             pltpu.SMEM((steps,), jnp.int32),

time: 46.6 us -> 44.5 us (0.955)
  Pallas kernels: 14.1 us -> 12 us
    pallas_call x1, Pallas kernels: 9.93 us -> 7.8 us  [score(): pl.pallas_call(functools.partial(score_kernel, places, sizes, direct), ou...]
where the time goes in v6:
time: 44.5 us; the launch traced here: 44.1 us
  blocking collectives  31.4 us (71%)
  Pallas kernels  12 us (27%)
  between operations  0.65 us (1%)
    all_to_all x1, blocking collectives, local(): message = lax.all_to_all(message, ALL, 0, 0, tiled=True)  21.7 us
    all_to_all x1, blocking collectives, local(): lax.all_to_all(gains, ALL, 0, 0, tiled=True)  9.77 us
    pallas_call x1, Pallas kernels, score(): pl.pallas_call(functools.partial(score_kernel, places, sizes, direct), ou...  7.8 us
    pallas_call x1, Pallas kernels, local(): pl.pallas_call(functools.partial(sort_kernel, (blocks, trees, own, rows,...  2.84 us
    pallas_call x1, Pallas kernels, local(): pl.pallas_call(functools.partial(finish_kernel, blocks, trees, own), out_...  1.36 us

profile of v6, /device:TPU:0, one launch (start us, length us, event | category | flops | bytes accessed | tf_op | source)
XLA Modules:
  0.0 44.1 jit_solution(640143739185092865)
XLA Ops:
  0.6 2.8 %shard_map.59 = bf16[32,56,128]{2,1,0:T(8,128)(2,1)} custom-call(s32[1]{0:T(128)} %bitcast.1.leaf_ref, s32[1]{0:T(128)} %bitcast.here_ref, f32[8,4,16,1024]{3,2,1,0:T(8,128)} %bitcast.6, s32[1,1024]{1,0:T(1,128)} %bitcast.7, bf16[1,1024]{1,0:T(2,128)(2,1)} %refs_1_.1, s32[1,1024]{1,0:T(1,128)} %refs_2_.1), custom_call_target="tpu_custom_call" | custom-call | tf_op jit(solution)/shard_map/pallas_call | solution.py:284
  3.5 21.7 %all_to_all.10 = bf16[32,56,128]{2,1,0:T(8,128)(2,1)S(1)} all-to-all(bf16[32,56,128]{2,1,0:T(8,128)(2,1)} %shard_map.59), channel_id=1, replica_groups=mesh['rows'=4,'feat'=2,'leaf'=4] {'rows','feat','leaf'}, dimensions={0} | all-to-all | bytes 917504 | tf_op jit(solution)/shard_map/all_to_all | solution.py:308
  25.2 7.8 %shard_map.60 = f32[32,1,128]{2,1,0:T(1,128)S(1)} custom-call(s32[1]{0:T(128)} %bitcast.1.leaf_ref, s32[1]{0:T(128)} %bitcast.here_ref, bf16[8,4,56,128]{3,2,1,0:T(8,128)(2,1)S(1)} %bitcast.5), custom_call_target="tpu_custom_call" | custom-call | tf_op jit(solution)/shard_map/pallas_call | solution.py:254
  33.0 9.8 %all_to_all.11.msg_ref = f32[32,1,128]{2,1,0:T(1,128)} all-to-all(f32[32,1,128]{2,1,0:T(1,128)S(1)} %shard_map.60), channel_id=1, replica_groups=mesh['rows'=4,'feat'=2,'leaf'=4] {'rows','feat','leaf'}, dimensions={0} | all-to-all | bytes 32768 | tf_op jit(solution)/shard_map/all_to_all | solution.py:350
  42.7 1.4 %shard_map.61 = (f32[1,2,64]{2,1,0:T(2,128)}, f32[1,2]{1,0:T(1,128)}) custom-call(s32[1]{0:T(128)} %bitcast.here_ref, f32[32,1,128]{2,1,0:T(1,128)} %all_to_all.11.msg_ref), custom_call_target="tpu_custom_call" | custom-call | tf_op jit(solution)/shard_map/pallas_call | solution.py:342

commit v7 on v6

--- a/solution.py
+++ b/solution.py
@@ -22,7 +22,6 @@
 BF16 = jnp.bfloat16
 F32 = jnp.float32
 VMEM = pl.BlockSpec(memory_space=pltpu.VMEM)
-SMEM = pl.BlockSpec(memory_space=pltpu.SMEM)
 HBM = pl.BlockSpec(memory_space=pltpu.HBM)
 
 
@@ -32,6 +31,10 @@
     return jnp.clip(nearest + above + (B // 2 - 1), float(LOWEST), float(HIGHEST))
 
 
+def block_of_device():
+    return lax.axis_index("rows") * lax.axis_size("feat") + lax.axis_index("feat")
+
+
 def iota(shape, axis):
     return lax.broadcasted_iota(jnp.int32, shape, axis).astype(F32)
 
@@ -40,7 +43,7 @@
     return lax.dot_general(a, b, (((1,), (1,)), ((), ())), preferred_element_type=F32)
 
 
-def sort_kernel(sizes, leaf_ref, here_ref, feature_ref, *refs):
+def sort_kernel(sizes, feature_ref, *refs):
     label_ref, weight_ref, node_ref, out_ref, slab, labels, weights, nodes, held, ordered, packed, sems = refs
     blocks, trees, own, rows, chunks, piece = sizes
     devices = blocks * trees
@@ -51,7 +54,7 @@
                 (label_ref, labels),
                 (weight_ref, weights),
                 (node_ref, nodes),
-                (feature_ref.at[:, leaf_ref[0]], slab),
+                (feature_ref.at[:, lax.axis_index("leaf")], slab),
             ]
         )
     ]
@@ -100,7 +103,7 @@
         out_ref[d] = packed[d * deep : (d + 1) * deep, :].astype(BF16)
 
 
-def score_kernel(places, sizes, direct, leaf_ref, here_ref, msg_ref, gain_ref, message, target, spread, total, whole, low, high):
+def score_kernel(places, sizes, direct, msg_ref, gain_ref, message, target, spread, total, whole, low, high):
     blocks, chunks, trees, own = sizes
     feature_at, weight_at, node_at, label_at = places
     groups = blocks // GROUP
@@ -109,6 +112,7 @@
     copies = LANES // own
     tiles = -(-(HIGHEST + 1 - LOWEST) // copies)
     first_bin = HIGHEST + 1 - tiles * copies
+    firsts = range(0, tiles, 2)[::-1]
     message[...] = msg_ref[...].astype(F32)
     total[: C * depth, :] = jnp.zeros((C * depth, total.shape[1]), F32)
 
@@ -148,7 +152,7 @@
 
     def add(step, start, held, beside=None):
         start = pl.multiple_of(start * depth, 8)
-        for at, first in enumerate(range(0, tiles, 2)):
+        for at, first in enumerate(firsts):
             last = min(first + 2, tiles)
             below = [
                 jnp.minimum(jnp.maximum((bins + float(tile * copies + 1)) - spread[step], zero), one)
@@ -159,8 +163,7 @@
                 held[...], jnp.concatenate(below, axis=1), preferred_element_type=F32
             )
             if beside is not None:
-                for g in range(at, GROUP, -(-tiles // 2)):
-                    prepare(beside, g)
+                beside(at)
 
     def more(step, carry):
         def one_pass(p, inner):
@@ -181,37 +184,59 @@
         add(step, low[step], target.at[step])
         return carry
 
-    if steps <= UNROLLED:
-        for step in range(steps):
-            set_limits(step)
-        for g in range(GROUP):
-            prepare(0, g)
-        for step in range(steps):
-            add(step, low[step], target.at[step], step + 1 if step + 1 < steps else None)
-    else:
-        lax.fori_loop(0, steps, window, 0)
-    lax.fori_loop(0, steps, more, 0)
-
     def ratio(squares, sums):
         return squares / jnp.maximum(sums, 1.0)
 
     zeros = jnp.zeros((depth, LANES), F32)
-    whole_sum, whole_square = zeros, zeros
-    for c in range(C):
-        part = jnp.broadcast_to(total[c * depth : (c + 1) * depth, tiles * LANES - 1 :], (depth, LANES))
-        whole[c * depth : (c + 1) * depth, :] = part
-        whole_sum, whole_square = whole_sum + part, whole_square + part * part
-    whole_ratio = ratio(whole_square, whole_sum)
-    best = jnp.full((depth, LANES), -jnp.inf, F32)
-    for tile in range(tiles):
+
+    def set_whole():
+        sums, squares = zeros, zeros
+        for c in range(C):
+            part = jnp.broadcast_to(total[c * depth : (c + 1) * depth, tiles * LANES - 1 :], (depth, LANES))
+            whole[c * depth : (c + 1) * depth, :] = part
+            sums, squares = sums + part, squares + part * part
+        return ratio(squares, sums)
+
+    def gain_of(tile, whole_ratio):
         left_sum, right_sum, left_square, right_square = zeros, zeros, zeros, zeros
         for c in range(C):
             left = total[c * depth : (c + 1) * depth, tile * LANES : (tile + 1) * LANES]
             right = whole[c * depth : (c + 1) * depth, :] - left
             left_sum, left_square = left_sum + left, left_square + left * left
             right_sum, right_square = right_sum + right, right_square + right * right
-        gain = ratio(left_square, left_sum) + ratio(right_square, right_sum) - whole_ratio
-        best = jnp.maximum(best, gain)
+        return ratio(left_square, left_sum) + ratio(right_square, right_sum) - whole_ratio
+
+    found = []
+    if steps <= UNROLLED:
+        for step in range(steps):
+            set_limits(step)
+        for g in range(GROUP):
+            prepare(0, g)
+        for step in range(steps - 1):
+
+            def prepare_next(at, step=step):
+                for g in range(at, GROUP, len(firsts)):
+                    prepare(step + 1, g)
+
+            add(step, low[step], target.at[step], prepare_next)
+        lax.fori_loop(0, steps, more, 0)
+        ratios = []
+
+        def score_done(at):
+            if at == 0:
+                ratios.append(set_whole())
+            else:
+                first = firsts[at - 1]
+                found.extend(gain_of(tile, ratios[0]) for tile in range(first, min(first + 2, tiles)))
+
+        add(steps - 1, low[steps - 1], target.at[steps - 1], score_done)
+        score_done(len(firsts))
+    else:
+        lax.fori_loop(0, steps, window, 0)
+        lax.fori_loop(0, steps, more, 0)
+        whole_ratio = set_whole()
+        found.extend(gain_of(tile, whole_ratio) for tile in range(tiles))
+    best = functools.reduce(jnp.maximum, found)
     shift = own
     while shift < LANES:
         best = jnp.maximum(best, pltpu.roll(best, shift, 1))
@@ -220,10 +245,11 @@
         gain_ref[...] = best[:, :own]
         return
     piece = own // trees
+    me = lax.axis_index("leaf")
     lane = lax.broadcasted_iota(jnp.int32, (depth, LANES), 1)
     sent = best
     for leaf in range(trees):
-        moved = pltpu.roll(best, lax.rem((leaf_ref[0] - leaf) * piece + LANES, LANES), 1)
+        moved = pltpu.roll(best, lax.rem((me - leaf) * piece + LANES, LANES), 1)
         sent = jnp.where(lane // own % trees == leaf, moved, sent)
     for t in range(trees):
         line = jnp.where(lane[:1] < trees * own, sent[t * NODES : t * NODES + 1], sent[t * NODES + 1 : t * NODES + 2])
@@ -231,13 +257,14 @@
             gain_ref[block * trees + t] = line
 
 
-def finish_kernel(blocks, trees, own, here_ref, msg_ref, gain_ref, best_ref):
+def finish_kernel(blocks, trees, own, msg_ref, gain_ref, best_ref):
+    here = block_of_device()
     piece = own // trees
     half = trees * own
     lane = lax.broadcasted_iota(jnp.int32, (1, LANES), 1)
-    mine = msg_ref[here_ref[0] * trees]
+    mine = msg_ref[here * trees]
     for leaf in range(1, trees):
-        mine = jnp.where(lane // piece % trees == leaf, msg_ref[here_ref[0] * trees + leaf], mine)
+        mine = jnp.where(lane // piece % trees == leaf, msg_ref[here * trees + leaf], mine)
     top = msg_ref[0]
     for d in range(1, blocks * trees):
         top = jnp.maximum(top, msg_ref[d])
@@ -246,7 +273,7 @@
         best_ref[:, n : n + 1] = jnp.max(top[:, n * half : (n + 1) * half], axis=1, keepdims=True)
 
 
-def score(message, places, sizes, direct, leaf, here):
+def score(message, places, sizes, direct):
     blocks, chunks, trees, own = sizes
     depth = trees * NODES
     steps = blocks * chunks // GROUP
@@ -254,7 +281,7 @@
     return pl.pallas_call(
         functools.partial(score_kernel, places, sizes, direct),
         out_shape=jax.ShapeDtypeStruct((blocks * trees, 1, LANES) if direct else (depth, own), F32),
-        in_specs=[SMEM, SMEM, VMEM],
+        in_specs=[VMEM],
         out_specs=VMEM,
         scratch_shapes=[
             pltpu.VMEM(message.shape, F32),
@@ -266,15 +293,13 @@
             pltpu.SMEM((steps,), jnp.int32),
         ],
         compiler_params=pltpu.CompilerParams(vmem_limit_bytes=40 << 20),
-    )(leaf, here, message)
+    )(message)
 
 
 def local(features, labels, weights, nodes, *, blocks, trees):
     feature_total, rows = features.shape
     own = feature_total // (blocks * trees)
     devices = blocks * trees
-    leaf = lax.axis_index("leaf").reshape(1)
-    here = (lax.axis_index("rows") * lax.axis_size("feat") + lax.axis_index("feat")).reshape(1)
     chunks = rows // LANES
     split_features = own % trees == 0
     if split_features:
@@ -285,8 +310,6 @@
             functools.partial(sort_kernel, (blocks, trees, own, rows, chunks, piece)),
             out_shape=jax.ShapeDtypeStruct((devices, deep, LANES), BF16),
             in_specs=[
-                SMEM,
-                SMEM,
                 HBM,
                 HBM,
                 HBM,
@@ -304,7 +327,7 @@
                 pltpu.SemaphoreType.DMA((4,)),
             ],
             compiler_params=pltpu.CompilerParams(vmem_limit_bytes=60 << 20),
-        )(leaf, here, features.reshape(blocks, trees, own, rows), labels.reshape(1, rows), weights, nodes)
+        )(features.reshape(blocks, trees, own, rows), labels.reshape(1, rows), weights, nodes)
         message = lax.all_to_all(message, ALL, 0, 0, tiled=True)
         message = message.reshape(blocks, trees, deep, LANES)
         places = (
@@ -315,9 +338,9 @@
         )
     else:
         share = rows // trees
-        mine = lax.dynamic_slice_in_dim(features, leaf[0] * share, share, 1)
+        mine = lax.dynamic_slice_in_dim(features, lax.axis_index("leaf") * share, share, 1)
         binned = bin_index(mine).astype(BF16).reshape(devices, own * share)
-        quarter = lax.dynamic_slice_in_dim(labels, leaf[0] * share, share, 0)
+        quarter = lax.dynamic_slice_in_dim(labels, lax.axis_index("leaf") * share, share, 0)
         common = jnp.concatenate([weights[0], nodes[0].astype(BF16), quarter.astype(BF16)])
         message = jnp.concatenate([binned, jnp.broadcast_to(common, (devices, common.shape[0]))], axis=1)
         message = lax.all_to_all(message, ALL, 0, 0, tiled=True).reshape(blocks, trees, -1)
@@ -337,7 +360,7 @@
         )
     sizes = (blocks, chunks, trees, own)
     direct = split_features and NODES * trees * own == LANES
-    gains = score(message, places, sizes, direct, leaf, here)
+    gains = score(message, places, sizes, direct)
     if direct:
         return pl.pallas_call(
             functools.partial(finish_kernel, blocks, trees, own),
@@ -345,13 +368,13 @@
                 jax.ShapeDtypeStruct((1, NODES, trees * own), F32),
                 jax.ShapeDtypeStruct((1, NODES), F32),
             ),
-            in_specs=[SMEM, VMEM],
+            in_specs=[VMEM],
             out_specs=(pl.BlockSpec(), pl.BlockSpec()),
-        )(here, lax.all_to_all(gains, ALL, 0, 0, tiled=True))
+        )(lax.all_to_all(gains, ALL, 0, 0, tiled=True))
     outgoing = jnp.broadcast_to(gains.reshape(1, trees, NODES * own), (blocks, trees, NODES * own))
     scores = lax.all_to_all(outgoing.reshape(devices, NODES * own), ALL, 0, 0, tiled=True)
     scores = scores.reshape(blocks, trees, NODES, own)
-    block = lax.dynamic_index_in_dim(scores, here[0], 0, keepdims=False)
+    block = lax.dynamic_index_in_dim(scores, block_of_device(), 0, keepdims=False)
     if split_features:
         split_gain = block.reshape(trees, NODES, trees, own // trees).transpose(1, 2, 0, 3)
     else:

time: 44.5 us -> 43.8 us (0.984)
  Pallas kernels: 12 us -> 11.3 us
    pallas_call x1, Pallas kernels: 7.8 us -> 7.13 us  [score(): pl.pallas_call(functools.partial(score_kernel, places, sizes, direct), ou...]
where the time goes in v7:
time: 43.8 us; the launch traced here: 43.4 us
  blocking collectives  31.4 us (72%)
  Pallas kernels  11.3 us (26%)
  between operations  0.64 us (1%)
    all_to_all x1, blocking collectives, local(): message = lax.all_to_all(message, ALL, 0, 0, tiled=True)  21.7 us
    all_to_all x1, blocking collectives, local(): lax.all_to_all(gains, ALL, 0, 0, tiled=True)  9.77 us
    pallas_call x1, Pallas kernels, score(): pl.pallas_call(functools.partial(score_kernel, places, sizes, direct), ou...  7.13 us
    pallas_call x1, Pallas kernels, local(): pl.pallas_call(functools.partial(sort_kernel, (blocks, trees, own, rows,...  2.84 us
    pallas_call x1, Pallas kernels, local(): pl.pallas_call(functools.partial(finish_kernel, blocks, trees, own), out_...  1.36 us

profile of v7, /device:TPU:0, one launch (start us, length us, event | category | flops | bytes accessed | tf_op | source)
XLA Modules:
  0.0 43.4 jit_solution(8341939661964940403)
XLA Ops:
  0.6 2.8 %shard_map.59 = bf16[32,56,128]{2,1,0:T(8,128)(2,1)} custom-call(f32[8,4,16,1024]{3,2,1,0:T(8,128)} %bitcast.4, s32[1,1024]{1,0:T(1,128)} %bitcast.5, bf16[1,1024]{1,0:T(2,128)(2,1)} %refs_1_.1, s32[1,1024]{1,0:T(1,128)} %refs_2_.1), custom_call_target="tpu_custom_call" | custom-call | tf_op jit(solution)/shard_map/pallas_call | solution.py:309
  3.5 21.7 %all_to_all.10 = bf16[32,56,128]{2,1,0:T(8,128)(2,1)S(1)} all-to-all(bf16[32,56,128]{2,1,0:T(8,128)(2,1)} %shard_map.59), channel_id=1, replica_groups=mesh['rows'=4,'feat'=2,'leaf'=4] {'rows','feat','leaf'}, dimensions={0} | all-to-all | bytes 917504 | tf_op jit(solution)/shard_map/all_to_all | solution.py:331
  25.2 7.1 %shard_map.60 = f32[32,1,128]{2,1,0:T(1,128)S(1)} custom-call(bf16[8,4,56,128]{3,2,1,0:T(8,128)(2,1)S(1)} %bitcast.3), custom_call_target="tpu_custom_call" | custom-call | tf_op jit(solution)/shard_map/pallas_call | solution.py:281
  32.3 9.8 %all_to_all.11.msg_ref = f32[32,1,128]{2,1,0:T(1,128)} all-to-all(f32[32,1,128]{2,1,0:T(1,128)S(1)} %shard_map.60), channel_id=1, replica_groups=mesh['rows'=4,'feat'=2,'leaf'=4] {'rows','feat','leaf'}, dimensions={0} | all-to-all | bytes 32768 | tf_op jit(solution)/shard_map/all_to_all | solution.py:373
  42.1 1.4 %shard_map.61 = (f32[1,2,64]{2,1,0:T(2,128)}, f32[1,2]{1,0:T(1,128)}) custom-call(f32[32,1,128]{2,1,0:T(1,128)} %all_to_all.11.msg_ref), custom_call_target="tpu_custom_call" | custom-call | tf_op jit(solution)/shard_map/pallas_call | solution.py:365

commit v8 on v7

--- a/solution.py
+++ b/solution.py
@@ -265,9 +265,10 @@
     mine = msg_ref[here * trees]
     for leaf in range(1, trees):
         mine = jnp.where(lane // piece % trees == leaf, msg_ref[here * trees + leaf], mine)
-    top = msg_ref[0]
-    for d in range(1, blocks * trees):
-        top = jnp.maximum(top, msg_ref[d])
+    chains = [
+        functools.reduce(jnp.maximum, [msg_ref[block * trees + leaf] for block in range(blocks)]) for leaf in range(trees)
+    ]
+    top = functools.reduce(jnp.maximum, chains)
     for n in range(NODES):
         gain_ref[0, n : n + 1, :] = mine[:, n * half : (n + 1) * half]
         best_ref[:, n : n + 1] = jnp.max(top[:, n * half : (n + 1) * half], axis=1, keepdims=True)
@@ -323,7 +324,7 @@
                 pltpu.VMEM((1, rows), jnp.int32),
                 pltpu.VMEM((held + 16, rows), BF16),
                 pltpu.VMEM((chunks, held + 16, LANES), F32),
-                pltpu.VMEM((devices * deep, LANES), F32),
+                pltpu.VMEM(((devices + 1) * deep, LANES), F32),
                 pltpu.SemaphoreType.DMA((4,)),
             ],
             compiler_params=pltpu.CompilerParams(vmem_limit_bytes=60 << 20),

time: 43.8 us -> 43.8 us (level)
  no operation moved by 1% of the time
where the time goes in v8:
time: 43.8 us; the launch traced here: 43.4 us
  blocking collectives  31.4 us (72%)
  Pallas kernels  11.3 us (26%)
  between operations  0.64 us (1%)
    all_to_all x1, blocking collectives, local(): message = lax.all_to_all(message, ALL, 0, 0, tiled=True)  21.7 us
    all_to_all x1, blocking collectives, local(): lax.all_to_all(gains, ALL, 0, 0, tiled=True)  9.77 us
    pallas_call x1, Pallas kernels, score(): pl.pallas_call(functools.partial(score_kernel, places, sizes, direct), ou...  7.12 us
    pallas_call x1, Pallas kernels, local(): pl.pallas_call(functools.partial(sort_kernel, (blocks, trees, own, rows,...  2.84 us
    pallas_call x1, Pallas kernels, local(): pl.pallas_call(functools.partial(finish_kernel, blocks, trees, own), out_...  1.36 us

profile of v8, /device:TPU:0, one launch (start us, length us, event | category | flops | bytes accessed | tf_op | source)
XLA Modules:
  0.0 43.4 jit_solution(4684310341630814744)
XLA Ops:
  0.6 2.8 %shard_map.59 = bf16[32,56,128]{2,1,0:T(8,128)(2,1)} custom-call(f32[8,4,16,1024]{3,2,1,0:T(8,128)} %bitcast.4, s32[1,1024]{1,0:T(1,128)} %bitcast.5, bf16[1,1024]{1,0:T(2,128)(2,1)} %refs_1_.1, s32[1,1024]{1,0:T(1,128)} %refs_2_.1), custom_call_target="tpu_custom_call" | custom-call | tf_op jit(solution)/shard_map/pallas_call | solution.py:310
  3.5 21.7 %all_to_all.10 = bf16[32,56,128]{2,1,0:T(8,128)(2,1)S(1)} all-to-all(bf16[32,56,128]{2,1,0:T(8,128)(2,1)} %shard_map.59), channel_id=1, replica_groups=mesh['rows'=4,'feat'=2,'leaf'=4] {'rows','feat','leaf'}, dimensions={0} | all-to-all | bytes 917504 | tf_op jit(solution)/shard_map/all_to_all | solution.py:332
  25.2 7.1 %shard_map.60 = f32[32,1,128]{2,1,0:T(1,128)S(1)} custom-call(bf16[8,4,56,128]{3,2,1,0:T(8,128)(2,1)S(1)} %bitcast.3), custom_call_target="tpu_custom_call" | custom-call | tf_op jit(solution)/shard_map/pallas_call | solution.py:282
  32.3 9.8 %all_to_all.11.msg_ref = f32[32,1,128]{2,1,0:T(1,128)} all-to-all(f32[32,1,128]{2,1,0:T(1,128)S(1)} %shard_map.60), channel_id=1, replica_groups=mesh['rows'=4,'feat'=2,'leaf'=4] {'rows','feat','leaf'}, dimensions={0} | all-to-all | bytes 32768 | tf_op jit(solution)/shard_map/all_to_all | solution.py:374
  42.0 1.4 %shard_map.61 = (f32[1,2,64]{2,1,0:T(2,128)}, f32[1,2]{1,0:T(1,128)}) custom-call(f32[32,1,128]{2,1,0:T(1,128)} %all_to_all.11.msg_ref), custom_call_target="tpu_custom_call" | custom-call | tf_op jit(solution)/shard_map/pallas_call | solution.py:366

commit v9 on v8

--- a/solution.py
+++ b/solution.py
@@ -208,13 +208,15 @@
 
     found = []
     if steps <= UNROLLED:
-        for step in range(steps):
+        for step in range(min(2, steps)):
             set_limits(step)
         for g in range(GROUP):
             prepare(0, g)
         for step in range(steps - 1):
 
             def prepare_next(at, step=step):
+                if at == 0 and step + 2 < steps:
+                    set_limits(step + 2)
                 for g in range(at, GROUP, len(firsts)):
                     prepare(step + 1, g)
 

time: 43.8 us -> 43.8 us (level)
  no operation moved by 1% of the time
where the time goes in v9:
time: 43.8 us; the launch traced here: 43.4 us
  blocking collectives  31.4 us (72%)
  Pallas kernels  11.3 us (26%)
  between operations  0.64 us (1%)
    all_to_all x1, blocking collectives, local(): message = lax.all_to_all(message, ALL, 0, 0, tiled=True)  21.7 us
    all_to_all x1, blocking collectives, local(): lax.all_to_all(gains, ALL, 0, 0, tiled=True)  9.77 us
    pallas_call x1, Pallas kernels, score(): pl.pallas_call(functools.partial(score_kernel, places, sizes, direct), ou...  7.13 us
    pallas_call x1, Pallas kernels, local(): pl.pallas_call(functools.partial(sort_kernel, (blocks, trees, own, rows,...  2.84 us
    pallas_call x1, Pallas kernels, local(): pl.pallas_call(functools.partial(finish_kernel, blocks, trees, own), out_...  1.36 us

profile of v9, /device:TPU:0, one launch (start us, length us, event | category | flops | bytes accessed | tf_op | source)
XLA Modules:
  0.0 43.4 jit_solution(4684310341630814744)
XLA Ops:
  0.6 2.8 %shard_map.59 = bf16[32,56,128]{2,1,0:T(8,128)(2,1)} custom-call(f32[8,4,16,1024]{3,2,1,0:T(8,128)} %bitcast.4, s32[1,1024]{1,0:T(1,128)} %bitcast.5, bf16[1,1024]{1,0:T(2,128)(2,1)} %refs_1_.1, s32[1,1024]{1,0:T(1,128)} %refs_2_.1), custom_call_target="tpu_custom_call" | custom-call | tf_op jit(solution)/shard_map/pallas_call | solution.py:312
  3.5 21.7 %all_to_all.10 = bf16[32,56,128]{2,1,0:T(8,128)(2,1)S(1)} all-to-all(bf16[32,56,128]{2,1,0:T(8,128)(2,1)} %shard_map.59), channel_id=1, replica_groups=mesh['rows'=4,'feat'=2,'leaf'=4] {'rows','feat','leaf'}, dimensions={0} | all-to-all | bytes 917504 | tf_op jit(solution)/shard_map/all_to_all | solution.py:334
  25.2 7.1 %shard_map.60 = f32[32,1,128]{2,1,0:T(1,128)S(1)} custom-call(bf16[8,4,56,128]{3,2,1,0:T(8,128)(2,1)S(1)} %bitcast.3), custom_call_target="tpu_custom_call" | custom-call | tf_op jit(solution)/shard_map/pallas_call | solution.py:284
  32.3 9.8 %all_to_all.11.msg_ref = f32[32,1,128]{2,1,0:T(1,128)} all-to-all(f32[32,1,128]{2,1,0:T(1,128)S(1)} %shard_map.60), channel_id=1, replica_groups=mesh['rows'=4,'feat'=2,'leaf'=4] {'rows','feat','leaf'}, dimensions={0} | all-to-all | bytes 32768 | tf_op jit(solution)/shard_map/all_to_all | solution.py:376
  42.1 1.4 %shard_map.61 = (f32[1,2,64]{2,1,0:T(2,128)}, f32[1,2]{1,0:T(1,128)}) custom-call(f32[32,1,128]{2,1,0:T(1,128)} %all_to_all.11.msg_ref), custom_call_target="tpu_custom_call" | custom-call | tf_op jit(solution)/shard_map/pallas_call | solution.py:368
